TPU v7x, 128 devices: a whole 4x4x4 slice. The times are simulated.
128 devices in a mesh: patch: 16 (over x_lo, y, core), tensor: 8 (over z, x_hi).
Axes of the slice: x: 4 (x_hi: 2, x_lo: 2; x = x_hi * 2 + x_lo), y: 4, z: 4, core: 2. Of those that a mesh axis runs over, the one named last changes fastest.
Arguments:
- latent_first: bfloat16 [4096, 5120], P('patch', 'tensor'), may hold values from -6 to 6
- latent_second: bfloat16 [4096, 5120], P('patch', 'tensor'), may hold values from -6 to 6
- stale_keys: bfloat16 [4096, 3072], P('patch', 'tensor'), may hold values from -12 to 12, as said below
- stale_values: bfloat16 [4096, 3072], P('patch', 'tensor'), may hold values from -6 to 6
- w_query: bfloat16 [5120, 3072], P(None, 'tensor'), may hold values from -0.078125 to 0.078125
- w_key: bfloat16 [5120, 3072], P(None, 'tensor'), may hold values from -0.078125 to 0.078125
- w_value: bfloat16 [5120, 3072], P(None, 'tensor'), may hold values from -0.078125 to 0.078125
- w_output: bfloat16 [3072, 5120], P('tensor'), may hold values from -0.109375 to 0.109375
Outputs:
- out_first: bfloat16 [4096, 5120], P('patch', 'tensor')
- out_second: bfloat16 [4096, 5120], P('patch', 'tensor')
Inputs may be any that keep to these rules, and one draw needn't show every extreme that they name: `stale_keys`: cached keys of every head.
All inputs are finite; a program needn't handle non-finite values.
Results may differ from a plain program's by a relative error of at most 0.009.
Values may be sent and summed in bfloat16 or wider, within the bound.
A program may use at most 128 MiB of HBM per device.

v0:
```python
import jax
import jax.numpy as jnp
from jax import lax
from jax.sharding import PartitionSpec as P

HD = 128


big_negative = -1e30


def head_norm(mat, heads_here, head_size):
    shaped = mat.reshape(mat.shape[0], heads_here, head_size)
    scaled = shaped * lax.rsqrt(jnp.mean(shaped * shaped, axis=-1, keepdims=True) + 1e-06)
    return scaled.astype(jnp.bfloat16)


def update_state(state, query, keys, values, masked):
    peak, total, acc = state
    head_size = query.shape[2]
    scores = jnp.einsum("qhd,khd->hqk", query, keys, preferred_element_type=jnp.float32) / jnp.sqrt(
        jnp.float32(head_size)
    )
    scores = jnp.where(masked[None, None, :], big_negative, scores)
    new_peak = jnp.maximum(peak, jnp.max(scores, axis=-1))
    factor = jnp.exp(peak - new_peak)
    expo = jnp.exp(scores - new_peak[:, :, None])
    total = total * factor + jnp.sum(expo, axis=-1)
    weights = expo.astype(jnp.bfloat16)
    acc = acc * factor[:, :, None] + jnp.einsum(
        "hqk,khd->hqd", weights, values, preferred_element_type=jnp.float32
    )
    return (new_peak, total, acc)


def project_step(whole, w_query, w_key, w_value, head_size):
    heads_here = w_query.shape[1] // head_size
    wide = whole.astype(jnp.float32)
    normed = (wide * lax.rsqrt(jnp.mean(wide * wide, axis=-1, keepdims=True) + 1e-06)).astype(
        jnp.bfloat16
    )
    query = head_norm(
        jnp.dot(normed, w_query, preferred_element_type=jnp.float32), heads_here, head_size
    )
    keyed = head_norm(
        jnp.dot(normed, w_key, preferred_element_type=jnp.float32), heads_here, head_size
    )
    valued = (
        jnp.dot(normed, w_value, preferred_element_type=jnp.float32)
        .astype(jnp.bfloat16)
        .reshape(whole.shape[0], heads_here, head_size)
    )
    start_state = (
        jnp.full((heads_here, whole.shape[0]), big_negative, jnp.float32),
        jnp.zeros((heads_here, whole.shape[0]), jnp.float32),
        jnp.zeros((heads_here, whole.shape[0], head_size), jnp.float32),
    )
    no_mask = jnp.zeros((whole.shape[0],), bool)
    own_state = update_state(start_state, query, keyed, valued, no_mask)
    return (query, keyed, valued, own_state)


def finish(state, rows):
    peak, total, acc = state
    attended = acc / total[:, :, None]
    return jnp.transpose(attended, (1, 0, 2)).astype(jnp.bfloat16).reshape(rows, -1)


def shards(
    latent_first, latent_second, stale_keys, stale_values, w_query, w_key, w_value, w_output
):
    rows = latent_first.shape[0]
    head_size = HD
    heads_here = w_query.shape[1] // head_size
    own_start = lax.axis_index("patch") * rows
    whole_first, whole_second = (
        lax.all_gather(latent_first, "tensor", axis=1, tiled=True),
        lax.all_gather(latent_second, "tensor", axis=1, tiled=True),
    )
    query_one, keys_one, values_one, state_one = project_step(
        whole_first, w_query, w_key, w_value, head_size
    )
    query_two, keys_two, values_two, state_two = project_step(
        whole_second, w_query, w_key, w_value, head_size
    )
    keys_flat = keys_one.reshape(rows, heads_here * head_size)
    values_flat = values_one.reshape(rows, heads_here * head_size)

    def piece_mask(count):
        position = jnp.arange(count, dtype=jnp.int32)
        return (position >= own_start) & (position < own_start + rows)

    def split_heads(piece):
        return piece.reshape(piece.shape[0], heads_here, head_size)

    pieces = (
        lax.all_gather(stale_keys, "patch", axis=0, tiled=True),
        lax.all_gather(stale_values, "patch", axis=0, tiled=True),
    )
    masked = piece_mask(pieces[0].shape[0])
    state_one = update_state(
        state_one, query_one, split_heads(pieces[0]), split_heads(pieces[1]), masked
    )
    pieces = (
        lax.all_gather(keys_flat, "patch", axis=0, tiled=True),
        lax.all_gather(values_flat, "patch", axis=0, tiled=True),
    )
    masked = piece_mask(pieces[0].shape[0])
    state_two = update_state(
        state_two, query_two, split_heads(pieces[0]), split_heads(pieces[1]), masked
    )
    attended_one = finish(state_one, rows)
    attended_two = finish(state_two, rows)
    partial_one = jnp.dot(attended_one, w_output, preferred_element_type=jnp.float32)
    partial_two = jnp.dot(attended_two, w_output, preferred_element_type=jnp.float32)
    summed_one, summed_two = (
        lax.psum_scatter(
            partial_one.astype(jnp.bfloat16), "tensor", scatter_dimension=1, tiled=True
        ).astype(jnp.float32),
        lax.psum_scatter(
            partial_two.astype(jnp.bfloat16), "tensor", scatter_dimension=1, tiled=True
        ).astype(jnp.float32),
    )
    out_first = (latent_first.astype(jnp.float32) + summed_one).astype(jnp.bfloat16)
    out_second = (latent_second.astype(jnp.float32) + summed_two).astype(jnp.bfloat16)
    return (out_first, out_second)


def solution(mesh):
    in_specs = (
        P("patch", "tensor"),
        P("patch", "tensor"),
        P("patch", "tensor"),
        P("patch", "tensor"),
        P(None, "tensor"),
        P(None, "tensor"),
        P(None, "tensor"),
        P("tensor", None),
    )
    out_specs = (P("patch", "tensor"), P("patch", "tensor"))
    return jax.shard_map(shards, mesh=mesh, in_specs=in_specs, out_specs=out_specs, check_vma=False)
```

profile of v0, /device:TPU:0, one launch (start us, length us, event | category | flops | bytes accessed | tf_op | source)
XLA Modules:
  0.0 453.7 jit_solution(13858745500442805725)
XLA Ops:
  8.7 1.7 copy.49
  10.5 60.7 %all-gather.7.cloned.1.call-done = bf16[256,5120]{1,0:T(8,128)(2,1)} async-done(((bf16[256,640]{1,0:T(8,128)(2,1)}), bf16[256,5120]{1,0:T(8,128)(2,1)}) %all-gather.7.cloned.1.call-update) | async-done | bytes 2621456 | tf_op jit(solution)/shard_map/all_gather | solution.py:77
  71.2 2.3 fusion.12
  73.5 4.6 %fusion.65 = f32[256,384]{1,0:T(8,128)S(1)} fusion(bf16[5120,384]{1,0:T(8,128)(2,1)} %param.13, bf16[256,5120]{1,0:T(8,128)(2,1)} %all-gather.7.cloned.1.call-done, f32[256]{0:T(256)S(1)} %add_rsqrt_fusion.5), kind=kOutput, calls=%fused_computation.100 | convolution fusion | flops 1010565120 | bytes 6947840 | tf_op jit(solution)/shard_map/dot_general | solution.py:46
  79.9 1.9 multiply_convert_fusion
  81.8 4.4 convolution_convert_fusion.3
  87.1 3.9 fusion.67
  91.1 38.5 %all-gather.13.cloned.1.call-done = bf16[256,5120]{1,0:T(8,128)(2,1)} async-done(((bf16[256,640]{1,0:T(8,128)(2,1)}), bf16[256,5120]{1,0:T(8,128)(2,1)}) %all-gather.13.cloned.1.call-update) | async-done | bytes 2621456 | tf_op jit(solution)/shard_map/all_gather | solution.py:78
  129.6 2.3 fusion.14
  132.0 4.8 %fusion.62 = f32[256,384]{0,1:T(8,128)S(1)} fusion(bf16[5120,384]{1,0:T(8,128)(2,1)} %param.12, bf16[256,5120]{1,0:T(8,128)(2,1)} %all-gather.13.cloned.1.call-done, f32[256]{0:T(256)S(1)} %add_rsqrt_fusion.4), kind=kOutput, calls=%fused_computation.99 | convolution fusion | flops 1010565120 | bytes 6947840 | tf_op jit(solution)/shard_map/dot_general | solution.py:43
  136.9 1.9 fusion.60
  140.2 1.6 convolution_convert_fusion.2
  143.8 27.0 %all-gather.9.cloned.1.call-done = bf16[4096,384]{0,1:T(8,128)(2,1)} async-done(((bf16[256,384]{0,1:T(8,128)(2,1)}), bf16[4096,384]{0,1:T(8,128)(2,1)}) %all-gather.9.cloned.1.call-update) | async-done | bytes 3145744 | tf_op jit(solution)/shard_map/all_gather | solution.py:97
  170.8 8.3 %fusion.42 = f32[3,256,4096]{2,1,0:T(8,128)} fusion(bf16[4096,3,128]{0,2,1:T(8,128)(2,1)} %bitcast.118, f32[256,3,128]{0,2,1:T(8,128)S(1)} %bitcast.115, f32[256,3]{0,1:T(4,128)S(1)} %add_rsqrt_fusion.3), kind=kOutput, calls=%fused_computation.63 | convolution fusion | flops 805502976 | bytes 16124928 | tf_op jit(solution)/shard_map/qhd,khd->hqk/dot_general | solution.py:21
  179.1 30.0 %all-gather.15.cloned.1.call-done = bf16[4096,384]{1,0:T(8,128)(2,1)} async-done(((bf16[256,384]{1,0:T(8,128)(2,1)}), bf16[4096,384]{1,0:T(8,128)(2,1)}) %all-gather.15.cloned.1.call-update) | async-done | bytes 3145744 | tf_op jit(solution)/shard_map/all_gather | solution.py:105
  209.1 4.7 %copy.60 = bf16[4096,384]{0,1:T(8,128)(2,1)} copy(bf16[4096,384]{1,0:T(8,128)(2,1)} %all-gather.15.cloned.1.call-done) | data formatting | bytes 6291456 | tf_op jit(solution)/shard_map/all_gather | solution.py:105
  213.7 32.8 %all-gather.17.cloned.1.call-done = bf16[4096,384]{1,0:T(8,128)(2,1)} async-done(((bf16[256,384]{1,0:T(8,128)(2,1)}), bf16[4096,384]{1,0:T(8,128)(2,1)}) %all-gather.17.cloned.1.call-update) | async-done | bytes 3145744 | tf_op jit(solution)/shard_map/all_gather | solution.py:106
  246.5 4.7 %copy.63 = bf16[4096,384]{0,1:T(8,128)(2,1)} copy(bf16[4096,384]{1,0:T(8,128)(2,1)} %all-gather.17.cloned.1.call-done) | data formatting | bytes 6291456 | tf_op jit(solution)/shard_map/all_gather | solution.py:106
  251.2 8.3 %fusion.1 = (f32[3,256]{1,0:T(4,128)S(1)}, f32[3,256]{1,0:T(4,128)S(1)}, f32[3,256,4096]{2,1,0:T(8,128)S(1)}) fusion(pred[4096]{0:T(1024)(128)(4,1)S(1)} %fusion.44, f32[3,256,4096]{2,1,0:T(8,128)} %fusion.42, bf16[4096,3,128]{0,2,1:T(8,128)(2,1)} %bitcast.105, f32[256,3,128]{0,2,1:T(8,128)S(1)} %bitcast.110, f32[256,3]{0,1:T(4,128)S(1)} %add_rsqrt_fusion.1), kind=kOutput, calls=%fused_computation.5 | convolution fusion | flops 824375808 | bytes 28718080 | tf_op jit(solution)/shard_map/qhd,khd->hqk/dot_general | solution.py:21
  260.9 5.7 %fusion.4 = (f32[3,256]{1,0:T(4,128)S(1)}, f32[3,256]{1,0:T(4,128)S(1)}) fusion(f32[3,256,4096]{2,1,0:T(8,128)S(1)} %get-tuple-element.18, f32[3,256]{1,0:T(4,128)S(1)} %get-tuple-element.12, pred[4096]{0:T(1024)(128)(4,1)S(1)} %fusion.44, f32[3,256]{1,0:T(4,128)S(1)} %get-tuple-element.15, f32[3,256,4096]{2,1,0:T(8,128)S(1)} %bitcast.104), kind=kLoop, calls=%fused_computation.8 | loop fusion | flops 25164288 | bytes 25182208 | tf_op jit(solution)/shard_map/reduce_sum | solution.py:28
  266.6 5.5 %fusion.27 = f32[256,3,128]{0,2,1:T(8,128)} fusion(bf16[4096,3,128]{0,2,1:T(8,128)(2,1)} %bitcast.116, f32[3,256,4096]{2,1,0:T(8,128)S(1)} %get-tuple-element.18, f32[3,256]{1,0:T(4,128)S(1)} %get-tuple-element.12, pred[4096]{0:T(1024)(128)(4,1)S(1)} %fusion.44), kind=kOutput, calls=%fused_computation.37 | convolution fusion | flops 817889280 | bytes 16129024 | tf_op jit(solution)/shard_map/hqk,khd->hqd/dot_general | solution.py:30
  272.1 1.5 fusion.31
  273.6 3.7 convolution_convert_fusion
  277.3 2.6 copy.79
  280.2 3.8 all-gather.11.cloned.1.call-done
  283.9 3.2 copy.52
  287.1 1.3 fusion.32
  288.4 6.6 %fusion.24 = f32[256,3,128]{0,2,1:T(8,128)S(1)} fusion(bf16[4096,3,128]{0,2,1:T(8,128)(2,1)S(1)} %bitcast.117, f32[3,256,4096]{2,1,0:T(8,128)} %fusion.42, f32[3,256]{1,0:T(4,128)S(1)} %get-tuple-element.15, pred[4096]{0:T(1024)(128)(4,1)S(1)} %fusion.44), kind=kOutput, calls=%fused_computation.36 | convolution fusion | flops 817889280 | bytes 16129024 | tf_op jit(solution)/shard_map/hqk,khd->hqd/dot_general | solution.py:30
  295.4 1.5 convolution_convert_fusion.1
  296.9 2.6 copy.77
  299.5 65.1 %reduce-scatter.9.cloned.1.call-done = bf16[640,256]{1,0:T(8,128)(2,1)} async-done(((bf16[5120,256]{1,0:T(8,128)(2,1)}), bf16[640,256]{1,0:T(8,128)(2,1)}) %reduce-scatter.9.cloned.1.call-update) | async-done | bytes 327696
  366.6 78.3 %reduce-scatter.7.cloned.1.call-done = bf16[640,256]{1,0:T(8,128)(2,1)} async-done(((bf16[5120,256]{1,0:T(8,128)(2,1)}), bf16[640,256]{1,0:T(8,128)(2,1)}) %reduce-scatter.7.cloned.1.call-update) | async-done | bytes 327696
  (73 shorter events, 13.4 us)
Async XLA Ops:
  7.2 64.0 %all-gather.7.cloned.1.call-start = ((), (), s32[]{:S(2)}) async-start(), calls=%async_computation.2 | async-start | bytes 2949120 | tf_op jit(solution)/shard_map/all_gather | solution.py:77
  7.9 121.7 %all-gather.13.cloned.1.call-start = ((), (), s32[]{:S(2)}) async-start(), calls=%async_computation.5 | async-start | bytes 2949120 | tf_op jit(solution)/shard_map/all_gather | solution.py:78
  8.6 162.2 %all-gather.9.cloned.1.call-start = ((), (), s32[]{:S(2)}) async-start(), calls=%async_computation.3 | async-start | bytes 3342336 | tf_op jit(solution)/shard_map/all_gather | solution.py:97
  10.5 198.6 %all-gather.15.cloned.1.call-start = ((), (), s32[]{:S(2)}) async-start(), calls=%async_computation.6 | async-start | bytes 3342336 | tf_op jit(solution)/shard_map/all_gather | solution.py:105
  73.5 8.3 %copy-start.3 = (bf16[256,5120]{1,0:T(8,128)(2,1)S(1)}, bf16[256,5120]{1,0:T(8,128)(2,1)}, u32[]{:S(2)}) copy-start(bf16[256,5120]{1,0:T(8,128)(2,1)} %all-gather.7.cloned.1.call-done) | copy-start | bytes 7864324
  78.2 0.8 copy-start.4
  81.8 164.7 %all-gather.17.cloned.1.call-start = ((), (), s32[]{:S(2)}) async-start(), calls=%async_computation.7 | async-start | bytes 3342336 | tf_op jit(solution)/shard_map/all_gather | solution.py:106
  86.3 197.6 %all-gather.11.cloned.1.call-start = ((), (), s32[]{:S(2)}) async-start(), calls=%async_computation.4 | async-start | bytes 3342336 | tf_op jit(solution)/shard_map/all_gather | solution.py:98
  86.9 277.8 %reduce-scatter.9.cloned.1.call-start = ((), (), s32[]{:S(2)}) async-start(), calls=%async_computation.9 | async-start | bytes 2949120
  132.0 4.9 %copy-start.2 = (bf16[256,5120]{1,0:T(8,128)(2,1)S(1)}, bf16[256,5120]{1,0:T(8,128)(2,1)}, u32[]{:S(2)}) copy-start(bf16[256,5120]{1,0:T(8,128)(2,1)} %all-gather.13.cloned.1.call-done) | copy-start | bytes 7864324
  132.0 4.9 %copy-start.9 = (bf16[5120,384]{1,0:T(8,128)(2,1)S(1)}, bf16[5120,384]{1,0:T(8,128)(2,1)}, u32[]{:S(2)}) copy-start(bf16[5120,384]{1,0:T(8,128)(2,1)} %param.13) | copy-start | bytes 11796484
  136.9 3.3 copy-start.10
  251.2 9.6 %slice-start = ((s8[12582912]{0:T(1024)(128)(4,1)}), s8[4194304]{0:T(1024)(128)(4,1)S(1)}, s32[]{:S(2)}) async-start(s8[12582912]{0:T(1024)(128)(4,1)} %bitcast.103), calls=%async_computation.10 | async-start | bytes 8388608
  251.2 9.6 %slice-start.1 = ((s8[12582912]{0:T(1024)(128)(4,1)}), s8[4194304]{0:T(1024)(128)(4,1)S(1)}, s32[]{:S(2)}) async-start(s8[12582912]{0:T(1024)(128)(4,1)} %bitcast.103), calls=%async_computation.11 | async-start | bytes 8388608
  251.2 9.6 %slice-start.2 = ((s8[12582912]{0:T(1024)(128)(4,1)}), s8[4194304]{0:T(1024)(128)(4,1)S(1)}, s32[]{:S(2)}) async-start(s8[12582912]{0:T(1024)(128)(4,1)} %bitcast.103), calls=%async_computation.12 | async-start | bytes 8388608
  266.6 5.5 %copy-start.8 = (bf16[256,384]{0,1:T(8,128)(2,1)S(1)}, bf16[256,384]{0,1:T(8,128)(2,1)}, u32[]{:S(2)}) copy-start(bf16[256,384]{0,1:T(8,128)(2,1)} %copy.57) | copy-start | bytes 589828
  277.3 2.7 copy-start.7
  279.9 165.0 %reduce-scatter.7.cloned.1.call-start = ((), (), s32[]{:S(2)}) async-start(), calls=%async_computation.8 | async-start | bytes 2949120
  288.4 6.7 %copy-start.1 = (f32[3,256,256]{1,2,0:T(8,128)S(1)}, f32[3,256,256]{1,2,0:T(8,128)}, u32[]{:S(2)}) copy-start(f32[3,256,256]{1,2,0:T(8,128)} %get-tuple-element.17) | copy-start | bytes 2359300
  288.4 6.9 %copy-start = (bf16[384,5120]{1,0:T(8,128)(2,1)S(1)}, bf16[384,5120]{1,0:T(8,128)(2,1)}, u32[]{:S(2)}) copy-start(bf16[384,5120]{1,0:T(8,128)(2,1)} %param.15) | copy-start | bytes 11796484
  296.9 68.9 %copy-start.5 = (bf16[256,640]{1,0:T(8,128)(2,1)S(1)}, bf16[256,640]{1,0:T(8,128)(2,1)}, u32[]{:S(2)}) copy-start(bf16[256,640]{1,0:T(8,128)(2,1)} %param.9) | copy-start | bytes 983044
  296.9 149.2 %copy-start.6 = (bf16[256,640]{1,0:T(8,128)(2,1)S(1)}, bf16[256,640]{1,0:T(8,128)(2,1)}, u32[]{:S(2)}) copy-start(bf16[256,640]{1,0:T(8,128)(2,1)} %param.8) | copy-start | bytes 983044
Sparse Core Ops, SparseCore 0:
  10.4 60.7 all-gather.6
  73.6 56.0 all-gather.12
  131.8 38.9 all-gather.8
  173.0 36.0 all-gather.14
  210.6 35.8 all-gather.16
  248.0 35.8 all-gather.10
  287.7 76.8 reduce-scatter.8
  368.4 76.4 reduce-scatter.6
where the time goes:
time: 454 us
  waiting for transfers between devices  338 us (74%)
  matrix products  59.5 us (13%)
  local copies, waits for them, and re-layouts  24.5 us (5%)
  other arithmetic  16.6 us (4%)
  between operations  14.5 us (3%)
    unnamed x10, waiting for transfers between devices  145 us
    all_gather x1, waiting for transfers between devices, shards(): lax.all_gather(latent_first, 'tensor', axis=1, tiled=True)  60.7 us
    all_gather x1, waiting for transfers between devices, shards(): lax.all_gather(latent_second, 'tensor', axis=1, tiled=True)  38.5 us
    all_gather x1, waiting for transfers between devices, shards(): lax.all_gather(values_flat, 'patch', axis=0, tiled=True)  32.8 us
    all_gather x1, waiting for transfers between devices, shards(): lax.all_gather(keys_flat, 'patch', axis=0, tiled=True)  30 us
    all_gather x1, waiting for transfers between devices, shards(): lax.all_gather(stale_keys, 'patch', axis=0, tiled=True)  27 us
    dot_general x4, matrix products, update_state(): jnp.einsum('qhd,khd->hqk', query, keys, preferred_element_type=jnp.float32)  19.1 us
    dot_general x4, matrix products, update_state(): jnp.einsum('hqk,khd->hqd', weights, values, preferred_element_type=jnp.fl...  13.9 us
  transfers between devices with their start and end apart: 8, of which 8 were waited for; matrix products, arithmetic and copies ran while one was open for 22% of the time, Pallas kernels for 0%

commit v1 on v0

v1 whole, which is shorter than its diff:
```python
import functools
import math

import jax
import jax.numpy as jnp
from jax import lax
from jax.experimental import pallas as pl
from jax.experimental.pallas import tpu as pltpu
from jax.sharding import PartitionSpec as P

HD = 128
EPS = 1e-06
C = math.log2(math.e) / math.sqrt(HD)
BF = jnp.bfloat16
F32 = jnp.float32
Y_ORDER = (1, 3, 2)


def _dot(a, b):
    return jnp.dot(a, b, preferred_element_type=F32)


def _dot_nt(a, b):
    return lax.dot_general(a, b, (((1,), (1,)), ((), ())), preferred_element_type=F32)


def _kernel(
    lat1, lat2, sk, sv, wq, wk, wv, wo,
    out1, out2,
    X, W, ACC, SS, QG, KB, VB, OWN, PS, PR, ST, STR, AG, WOG, OACC, A2, L2,
    x_s, x_r, w_l, c_s, c_r, n_s, n_r, q_s, q_r, p_s, p_r, t_s, t_r, a_s, a_r,
    o1_s, o1_r, o2_s, o2_r, o3_s, o3_r, l_s,
):
    lats = (lat1, lat2)
    patch = lax.axis_index("patch")
    tens = lax.axis_index("tensor")
    xl, y, c = patch // 8, (patch // 2) % 4, patch % 2
    z, xh = tens // 2, tens % 2

    def y_peer(d):
        return (xl * 8 + ((y + d) % 4) * 2 + c, tens)

    def class_peer(j):
        nc = (c + j % 2) % 2
        nx = (xl + j // 2) % 2
        return (nx * 8 + y * 2 + nc, tens)

    def t_index(r):
        return ((z + r // 2) % 4) * 2 + (xh + r % 2) % 2

    def t_peer(r):
        return (patch, t_index(r))

    def mirror(r):
        return ((4 - r // 2) % 4) * 2 + r % 2

    def remote(src, dst, ssem, rsem, dev):
        return pltpu.make_async_remote_copy(
            src_ref=src, dst_ref=dst, send_sem=ssem, recv_sem=rsem,
            device_id=dev, device_id_type=pl.DeviceIdType.MESH,
        )

    T_ORDER = (1, 2, 6, 3, 7, 4, 5)
    sends = []

    bar = pltpu.get_barrier_semaphore()
    peers = [y_peer(d) for d in Y_ORDER] + [class_peer(j) for j in (1, 2, 3)] + [t_peer(r) for r in range(1, 8)]
    for dev in peers:
        pl.semaphore_signal(bar, inc=1, device_id=dev, device_id_type=pl.DeviceIdType.MESH)
    pl.semaphore_wait(bar, len(peers))

    def start_latents(s):
        for r in T_ORDER:
            cp = remote(lats[s], X.at[s, mirror(r)], x_s.at[s, r], x_r.at[s, mirror(r)], t_peer(r))
            cp.start()
            sends.append(cp)

    start_latents(0)
    own_lat = [pltpu.make_async_copy(lats[s], X.at[s, 0], x_r.at[s, 0]) for s in (0, 1)]
    for cp in own_lat:
        cp.start()

    own_k = pltpu.make_async_copy(sk, KB.at[0, pl.ds(1024, 256)], l_s.at[0])
    own_v = pltpu.make_async_copy(sv, VB.at[0, pl.ds(1024, 256)], l_s.at[1])
    own_k.start()
    own_v.start()
    for d in Y_ORDER:
        r = 4 - d
        for i, (src, buf) in enumerate(((sk, KB), (sv, VB))):
            cp = remote(src, buf.at[0, pl.ds(r * 256, 256)], c_s.at[i, d], c_r.at[i, r], y_peer(d))
            cp.start()
            sends.append(cp)

    for i in range(8):
        r = (0,) + T_ORDER
        r = r[i]
        rows = pl.ds(pl.multiple_of(t_index(r) * 640, 640), 640)
        for k, w in enumerate((wq, wk, wv)):
            pltpu.make_async_copy(w.at[rows], W.at[r, :, pl.ds(k * 384, 384)], w_l.at[r, k]).start()

    own_cols = pl.ds(pl.multiple_of(tens * 640, 640), 640)
    own_wo = pltpu.make_async_copy(wo.at[:, :, own_cols], WOG.at[:, 0], l_s.at[2])
    own_wo.start()

    def project(s):
        ACC[...] = jnp.zeros_like(ACC)
        SS[...] = jnp.zeros_like(SS)

        def chunk(i, carry):
            r = jnp.where(i < 3, i, jnp.where(i == 3, 6, jnp.where(i == 4, 3, jnp.where(i == 5, 7, i - 2))))
            remote(lats[s], X.at[s, r], x_s.at[s, 0], x_r.at[s, r], t_peer(1)).wait_recv()
            if s == 0:
                for k, w in enumerate((wq, wk, wv)):
                    pltpu.make_async_copy(
                        w.at[pl.ds(0, 640)], W.at[r, :, pl.ds(k * 384, 384)], w_l.at[r, k]
                    ).wait()
            x = X[s, r]
            xf = x.astype(F32)
            sq = xf * xf
            SS[...] += sq[:, :128] + sq[:, 128:256] + sq[:, 256:384] + sq[:, 384:512] + sq[:, 512:640]
            ACC[...] += _dot(x, W[r])
            return carry

        lax.fori_loop(0, 8, chunk, 0)

    def norms(s):
        inv = lax.rsqrt(jnp.sum(SS[...], axis=-1, keepdims=True) * (1.0 / 5120) + EPS)
        for h in range(3):
            cols = pl.ds(h * 128, 128)
            k = ACC[:, pl.ds(384 + h * 128, 128)] * inv
            k = (k * lax.rsqrt(jnp.mean(k * k, axis=-1, keepdims=True) + EPS)).astype(BF)
            KB[s, pl.ds(0, 256), cols] = k
            v = (ACC[:, pl.ds(768 + h * 128, 128)] * inv).astype(BF)
            VB[s, pl.ds(0, 256), cols] = v
            if s == 0:
                KB[1, pl.ds(1024, 256), cols] = k
                VB[1, pl.ds(1024, 256), cols] = v
        if s == 0:
            for d in Y_ORDER:
                r = 4 - d
                for i, buf in enumerate((KB, VB)):
                    cp = remote(
                        buf.at[1, pl.ds(1024, 256)], buf.at[1, pl.ds(r * 256, 256)],
                        n_s.at[i, d], n_r.at[i, r], y_peer(d),
                    )
                    cp.start()
                    sends.append(cp)
        for h in range(3):
            cols = pl.ds(h * 128, 128)
            q = ACC[:, cols] * inv
            QG[s, 0, :, cols] = (q * lax.rsqrt(jnp.mean(q * q, axis=-1, keepdims=True) + EPS)).astype(BF)
        for j in (3, 2, 1):
            cp = remote(QG.at[s, 0], QG.at[s, j], q_s.at[s, j], q_r.at[s, j], class_peer(j))
            cp.start()
            sends.append(cp)

    def wait_queries(s):
        for j in (1, 2, 3):
            remote(QG.at[s, 0], QG.at[s, j], q_s.at[s, j], q_r.at[s, j], class_peer(j)).wait_recv()

    lane = lax.broadcasted_iota(jnp.int32, (256, 128), 1)

    def send_partials(s, h):
        for j in (3, 2, 1):
            cp = remote(PS.at[s, h, j], PR.at[s, h, j], p_s.at[s, h, j], p_r.at[s, h, j], class_peer(j))
            cp.start()
            sends.append(cp)
            cp = remote(ST.at[s, h, j], STR.at[s, h, j], t_s.at[s, h, j], t_r.at[s, h, j], class_peer(j))
            cp.start()
            sends.append(cp)

    def attention_one():
        for h in range(3):
            cols = pl.ds(h * 128, 128)

            def per_class(j, carry):
                start = pl.multiple_of(jnp.where(j == 0, 0, 256), 256)
                q = QG[0, j, :, cols]
                sc = _dot_nt(q, KB[0, pl.ds(start, 1024), cols])
                m = jnp.max(sc, axis=-1, keepdims=True)
                p = jnp.exp2((sc - m) * C)
                l = jnp.sum(p, axis=-1, keepdims=True)
                a = _dot(p.astype(BF), VB[0, pl.ds(start, 1024), cols])
                PS[0, h, j] = a.astype(BF)
                both = jnp.where(lane == 0, l, m)
                ST[0, h, j] = both.T[:8]

                @pl.when(j == 0)
                def _():
                    OWN[h] = a

                return carry

            lax.fori_loop(0, 4, per_class, 0)
            send_partials(0, h)

    def attention_two(part):
        first = part == 0
        for h in range(3):
            cols = pl.ds(h * 128, 128)
            if first:
                blocks = ((0, 1, 0), (1, 3, 1024))
            else:
                blocks = ((0, 4, part * 256),)
            for j0, nj, row in blocks:
                q = QG[1, pl.ds(j0, nj), :, cols].reshape(nj * 256, 128)
                p = jnp.exp2(_dot_nt(q, KB[1, pl.ds(row, 256), cols]) * C)
                l = p[:, :128] + p[:, 128:]
                a = _dot(p.astype(BF), VB[1, pl.ds(row, 256), cols])
                rows = pl.ds(j0 * 256, nj * 256)
                if first:
                    A2[h, rows] = a
                    L2[h, rows] = l
                else:
                    A2[h, rows] += a
                    L2[h, rows] += l
            if part == Y_ORDER[-1]:
                OWN[h] = A2[h, pl.ds(0, 256)]
                for j in range(4):
                    rows = pl.ds(j * 256, 256)
                    PS[1, h, j] = A2[h, rows].astype(BF)
                    l = jnp.sum(L2[h, rows], axis=-1, keepdims=True)
                    ST[1, h, j] = jnp.broadcast_to(l, (256, 128)).T[:8]
                send_partials(1, h)

    def merge(s, h):
        for j in (1, 2, 3):
            remote(PS.at[s, h, j], PR.at[s, h, j], p_s.at[s, h, j], p_r.at[s, h, j], class_peer(j)).wait_recv()
            remote(ST.at[s, h, j], STR.at[s, h, j], t_s.at[s, h, j], t_r.at[s, h, j], class_peer(j)).wait_recv()
        stats = [ST[s, h, 0]] + [STR[s, h, j] for j in (1, 2, 3)]
        cols = [jnp.concatenate([st] * 16, axis=0).T for st in stats]
        accs = [OWN[h]] + [PR[s, h, j].astype(F32) for j in (1, 2, 3)]
        ls = [st[:, 0:1] for st in cols]
        if s == 0:
            ms = [st[:, 1:2] for st in cols]
            top = functools.reduce(jnp.maximum, ms)
            ws = [jnp.exp2((m - top) * C) for m in ms]
            total = sum(w * l for w, l in zip(ws, ls))
            acc = sum(w * a for w, a in zip(ws, accs))
        else:
            total = sum(ls)
            acc = sum(accs)
        AG[s, h, :, pl.ds(0, 128)] = (acc / total).astype(BF)
        for r in T_ORDER:
            m = mirror(r)
            cp = remote(
                AG.at[s, h, :, pl.ds(0, 128)], AG.at[s, h, :, pl.ds(m * 128, 128)],
                a_s.at[s, h, r], a_r.at[s, h, m], t_peer(r),
            )
            cp.start()
            sends.append(cp)

    def out_head(s, h):
        for r in T_ORDER:
            remote(
                AG.at[s, h, :, pl.ds(0, 128)], AG.at[s, h, :, pl.ds(r * 128, 128)],
                a_s.at[s, h, r], a_r.at[s, h, r], t_peer(r),
            ).wait_recv()
        part = _dot(AG[s, h], WOG[h].reshape(1024, 640))
        if h == 0:
            OACC[...] = part + X[s, 0].astype(F32)
        elif h == 1:
            OACC[...] += part
        else:
            (out1, out2)[s][...] = (OACC[...] + part).astype(BF)

    def wo_rows(yy):
        return pl.ds(pl.multiple_of((((y + yy) % 4) * 2 + c) * 16, 16), 16)

    def wo_first():
        for r in T_ORDER:
            m = mirror(r)
            cols = pl.ds(pl.multiple_of(t_index(r) * 640, 640), 640)
            cp = remote(wo.at[:, wo_rows(0), cols], WOG.at[:, m, wo_rows(0)], o1_s.at[r], o1_r.at[m], t_peer(r))
            cp.start()
            sends.append(cp)

    def wo_first_wait():
        for r in T_ORDER:
            remote(
                wo.at[:, wo_rows(0), pl.ds(0, 640)], WOG.at[:, r, wo_rows(0)], o1_s.at[r], o1_r.at[r], t_peer(r)
            ).wait_recv()

    def wo_piece(yy):
        return WOG.at[:, pl.ds(1, 7), wo_rows(yy)]

    def wo_third(yy):
        cp = remote(wo_piece(yy), wo_piece(yy), o3_s.at[yy], o3_r.at[yy], class_peer(1))
        cp.start()
        sends.append(cp)

    def wo_second():
        for d in Y_ORDER:
            cp = remote(wo_piece(0), wo_piece(0), o2_s.at[d], o2_r.at[4 - d], y_peer(d))
            cp.start()
            sends.append(cp)
        wo_third(0)

    def wo_relay():
        for r in Y_ORDER:
            remote(wo_piece(0), wo_piece(r), o2_s.at[r], o2_r.at[r], y_peer(r)).wait_recv()
            wo_third(r)

    def wo_last_wait():
        for yy in range(4):
            rows = pl.ds(pl.multiple_of((((y + yy) % 4) * 2 + (1 - c)) * 16, 16), 16)
            piece = WOG.at[:, pl.ds(1, 7), rows]
            remote(piece, piece, o3_s.at[yy], o3_r.at[yy], class_peer(1)).wait_recv()
        own_wo.wait()

    project(0)
    start_latents(1)
    wo_first()
    norms(0)
    own_k.wait()
    own_v.wait()
    for r in Y_ORDER:
        for i, (src, buf) in enumerate(((sk, KB), (sv, VB))):
            remote(src, buf.at[0, pl.ds(r * 256, 256)], c_s.at[i, r], c_r.at[i, r], y_peer(r)).wait_recv()
    wait_queries(0)
    attention_one()
    wo_first_wait()
    wo_second()
    for h in range(3):
        merge(0, h)
    project(1)
    norms(1)
    wait_queries(1)
    attention_two(0)
    wo_relay()
    for r in Y_ORDER:
        for i, buf in enumerate((KB, VB)):
            remote(
                buf.at[1, pl.ds(1024, 256)], buf.at[1, pl.ds(r * 256, 256)],
                n_s.at[i, r], n_r.at[i, r], y_peer(r),
            ).wait_recv()
        attention_two(r)
    wo_last_wait()
    for h in range(3):
        merge(1, h)
        out_head(0, h)
    for h in range(3):
        out_head(1, h)
    for cp in sends:
        cp.wait_send()


def _shards(latent_first, latent_second, stale_keys, stale_values, w_query, w_key, w_value, w_output):
    dma = pltpu.SemaphoreType.DMA
    vm = pltpu.VMEM
    scratch = [
        vm((2, 8, 256, 640), BF),
        vm((8, 640, 1152), BF),
        vm((256, 1152), F32),
        vm((256, 128), F32),
        vm((2, 4, 256, 384), BF),
        vm((2, 1280, 384), BF),
        vm((2, 1280, 384), BF),
        vm((3, 256, 128), F32),
        vm((2, 3, 4, 256, 128), BF),
        vm((2, 3, 4, 256, 128), BF),
        vm((2, 3, 4, 8, 256), F32),
        vm((2, 3, 4, 8, 256), F32),
        vm((2, 3, 256, 1024), BF),
        vm((3, 8, 128, 640), BF),
        vm((256, 640), F32),
        vm((3, 1024, 128), F32),
        vm((3, 1024, 128), F32),
        dma((2, 8)), dma((2, 8)),
        dma((8, 3)),
        dma((2, 4)), dma((2, 4)),
        dma((2, 4)), dma((2, 4)),
        dma((2, 4)), dma((2, 4)),
        dma((2, 3, 4)), dma((2, 3, 4)),
        dma((2, 3, 4)), dma((2, 3, 4)),
        dma((2, 3, 8)), dma((2, 3, 8)),
        dma((8,)), dma((8,)),
        dma((4,)), dma((4,)),
        dma((4,)), dma((4,)),
        dma((3,)),
    ]
    out = jax.ShapeDtypeStruct((256, 640), BF)
    return pl.pallas_call(
        _kernel,
        out_shape=(out, out),
        in_specs=[pl.BlockSpec(memory_space=pl.ANY)] * 8,
        out_specs=(pl.BlockSpec(memory_space=pltpu.VMEM),) * 2,
        scratch_shapes=scratch,
        compiler_params=pltpu.CompilerParams(
            collective_id=0, has_side_effects=True, vmem_limit_bytes=60 * 2**20
        ),
        cost_estimate=pl.CostEstimate(flops=11_300_000_000, bytes_accessed=20_000_000, transcendentals=6_300_000),
        name="patch_attention",
    )(
        latent_first, latent_second, stale_keys, stale_values,
        w_query, w_key, w_value, w_output.reshape(3, 128, 5120),
    )


def solution(mesh):
    in_specs = (
        P("patch", "tensor"),
        P("patch", "tensor"),
        P("patch", "tensor"),
        P("patch", "tensor"),
        P(None, "tensor"),
        P(None, "tensor"),
        P(None, "tensor"),
        P("tensor", None),
    )
    out_specs = (P("patch", "tensor"), P("patch", "tensor"))
    return jax.shard_map(_shards, mesh=mesh, in_specs=in_specs, out_specs=out_specs, check_vma=False)
```

time: 454 us -> 163 us (0.36)
  waiting for transfers between devices: 338 us -> 0 us
  Pallas kernels: 0 us -> 158 us
  matrix products: 59.5 us -> 0 us
  local copies, waits for them, and re-layouts: 24.5 us -> 3.45 us
  other arithmetic: 16.6 us -> 0 us
  between operations: 14.5 us -> 0.64 us
    all_gather x6 -> x0, waiting for transfers between devices: 193 us -> none  [the longest x1 60.7 us: shards(): lax.all_gather(latent_first, 'tensor', axis=1, tiled=True)]
    pallas_call x0 -> x1, Pallas kernels: none -> 158 us  [_shards(): pl.pallas_call(_kernel, out_shape=(out, out), in_specs=[pl.BlockSpec(memo...]
    unnamed x10 -> x0, waiting for transfers between devices: 145 us -> none
    dot_general x16 -> x0, matrix products: 59.5 us -> none  [the longest x4 19.1 us: update_state(): jnp.einsum('qhd,khd->hqk', query, keys, preferred_element_type=jnp.float32)]
    reduce_sum x9 -> x0, other arithmetic: 13.1 us -> none  [the longest x3 8.2 us: update_state(): total = total * factor + jnp.sum(expo, axis=-1)]
    all_gather x3 -> x0, local copies, waits for them, and re-layouts: 12.6 us -> none  [the longest x1 4.73 us: shards(): lax.all_gather(values_flat, 'patch', axis=0, tiled=True)]
    unnamed x33 -> x2, local copies, waits for them, and re-layouts: 9.85 us -> 3.45 us
  transfers between devices with their start and end apart: 8 -> 0, of which waited for: 8 -> 0; matrix products, arithmetic and copies ran while one was open for 22% -> 0% of each run, Pallas kernels for 0% -> 0%
where the time goes in v1:
time: 163 us; the launch traced here: 162 us
  Pallas kernels  158 us (97%)
  local copies, waits for them, and re-layouts  3.45 us (2%)
    pallas_call x1, Pallas kernels, _shards(): pl.pallas_call(_kernel, out_shape=(out, out), in_specs=[pl.BlockSpec(memo...  158 us
    unnamed x2, local copies, waits for them, and re-layouts  3.45 us

profile of v1, /device:TPU:0, one launch (start us, length us, event | category | flops | bytes accessed | tf_op | source)
XLA Modules:
  0.0 162.4 jit_solution(18288478362795990153)
XLA Ops:
  0.6 158.3 %patch_attention.1 = (bf16[256,640]{1,0:T(8,128)(2,1)}, bf16[256,640]{1,0:T(8,128)(2,1)}) custom-call(bf16[256,640]{1,0:T(8,128)(2,1)} %lat1.1, bf16[256,640]{1,0:T(8,128)(2,1)} %lat2.1, bf16[256,384]{1,0:T(8,128)(2,1)} %sk.1, bf16[256,384]{1,0:T(8,128)(2,1)} %sv.1, bf16[5120,384]{1,0:T(8,128)(2,1)} %wq.1, bf16[5120,384]{1,0:T(8,128)(2,1)} %wk.1, ...), custom_call_target="tpu_custom_call" | custom-call | flops 11299999744 | bytes 20000000 | tf_op jit(solution)/shard_map/patch_attention/pallas_call | solution.py:383
  158.9 1.7 %copy.12 = bf16[256,640]{1,0:T(8,128)(2,1)} copy(bf16[256,640]{1,0:T(8,128)(2,1)} %get-tuple-element.4) | data formatting | bytes 655360
  160.7 1.7 %copy.13 = bf16[256,640]{1,0:T(8,128)(2,1)} copy(bf16[256,640]{1,0:T(8,128)(2,1)} %get-tuple-element.5) | data formatting | bytes 655360

commit v2 on v1

--- a/solution.py
+++ b/solution.py
@@ -61,7 +61,18 @@
         )
 
     T_ORDER = (1, 2, 6, 3, 7, 4, 5)
+    SLOTS = (0, 1, 4, 2, 6, 5, 3, 7)
     sends = []
+    pending = {}
+
+    def send(key, src, dst, ssem, rsem, dev, here, here_sem):
+        cp = remote(src, dst, ssem, rsem, dev)
+        cp.start()
+        sends.append(cp)
+        pending[key] = remote(here, here, here_sem, here_sem, t_peer(1))
+
+    def take(*key):
+        pending.pop(key).wait_recv()
 
     bar = pltpu.get_barrier_semaphore()
     peers = [y_peer(d) for d in Y_ORDER] + [class_peer(j) for j in (1, 2, 3)] + [t_peer(r) for r in range(1, 8)]
@@ -69,11 +80,36 @@
         pl.semaphore_signal(bar, inc=1, device_id=dev, device_id_type=pl.DeviceIdType.MESH)
     pl.semaphore_wait(bar, len(peers))
 
+    def gather_send(key, own, at, ssem, rsem):
+        for r in (1, 4, 2, 6):
+            m = mirror(r)
+            send(key + (r,), own, at(m), ssem(r), rsem(m), t_peer(r), at(r), rsem(r))
+
+    def gather_pass_partner(key, at, ssem, rsem):
+        take(*key, 1)
+        for r, slot in ((2, 7), (6, 3)):
+            send(key + (slot,), at(1), at(slot), ssem(slot), rsem(slot), t_peer(r), at(slot), rsem(slot))
+
+    def gather_pass_opposite(key, at, ssem, rsem):
+        take(*key, 4)
+        send(key + (5,), at(4), at(5), ssem(5), rsem(5), t_peer(1), at(5), rsem(5))
+
+    def latents_at(s):
+        return ("x", s), (lambda r: X.at[s, r]), (lambda r: x_s.at[s, r]), (lambda r: x_r.at[s, r])
+
     def start_latents(s):
-        for r in T_ORDER:
-            cp = remote(lats[s], X.at[s, mirror(r)], x_s.at[s, r], x_r.at[s, mirror(r)], t_peer(r))
-            cp.start()
-            sends.append(cp)
+        key, at, ssem, rsem = latents_at(s)
+        gather_send(key, lats[s], at, ssem, rsem)
+
+    def attended_at(s, h):
+        return (
+            ("a", s, h), (lambda r: AG.at[s, h, :, pl.ds(r * 128, 128)]),
+            (lambda r: a_s.at[s, h, r]), (lambda r: a_r.at[s, h, r]),
+        )
+
+    def start_attended(s, h):
+        key, at, ssem, rsem = attended_at(s, h)
+        gather_send(key, at(0), at, ssem, rsem)
 
     start_latents(0)
     own_lat = [pltpu.make_async_copy(lats[s], X.at[s, 0], x_r.at[s, 0]) for s in (0, 1)]
@@ -87,41 +123,47 @@
     for d in Y_ORDER:
         r = 4 - d
         for i, (src, buf) in enumerate(((sk, KB), (sv, VB))):
-            cp = remote(src, buf.at[0, pl.ds(r * 256, 256)], c_s.at[i, d], c_r.at[i, r], y_peer(d))
-            cp.start()
-            sends.append(cp)
-
-    for i in range(8):
-        r = (0,) + T_ORDER
-        r = r[i]
+            here = pl.ds(r * 256, 256)
+            send(("c", i, r), src, buf.at[0, here], c_s.at[i, d], c_r.at[i, r], y_peer(d), buf.at[0, here], c_r.at[i, r])
+
+    w_copies = {}
+    for r in SLOTS:
+        w_copies[r] = []
         rows = pl.ds(pl.multiple_of(t_index(r) * 640, 640), 640)
         for k, w in enumerate((wq, wk, wv)):
-            pltpu.make_async_copy(w.at[rows], W.at[r, :, pl.ds(k * 384, 384)], w_l.at[r, k]).start()
+            copy = pltpu.make_async_copy(w.at[rows], W.at[r, :, pl.ds(k * 384, 384)], w_l.at[r, k])
+            copy.start()
+            w_copies[r].append(copy)
 
     own_cols = pl.ds(pl.multiple_of(tens * 640, 640), 640)
     own_wo = pltpu.make_async_copy(wo.at[:, :, own_cols], WOG.at[:, 0], l_s.at[2])
     own_wo.start()
 
     def project(s):
-        ACC[...] = jnp.zeros_like(ACC)
-        SS[...] = jnp.zeros_like(SS)
-
-        def chunk(i, carry):
-            r = jnp.where(i < 3, i, jnp.where(i == 3, 6, jnp.where(i == 4, 3, jnp.where(i == 5, 7, i - 2))))
-            remote(lats[s], X.at[s, r], x_s.at[s, 0], x_r.at[s, r], t_peer(1)).wait_recv()
+        if s == 0:
+            gather_pass_partner(*latents_at(0))
+            gather_pass_opposite(*latents_at(0))
+        for r in SLOTS:
+            if r == 0:
+                own_lat[s].wait()
+            elif r not in (1, 4):
+                if s == 0 and r == SLOTS[-1]:
+                    start_latents(1)
+                take("x", s, r)
             if s == 0:
-                for k, w in enumerate((wq, wk, wv)):
-                    pltpu.make_async_copy(
-                        w.at[pl.ds(0, 640)], W.at[r, :, pl.ds(k * 384, 384)], w_l.at[r, k]
-                    ).wait()
+                for copy in w_copies[r]:
+                    copy.wait()
             x = X[s, r]
             xf = x.astype(F32)
             sq = xf * xf
-            SS[...] += sq[:, :128] + sq[:, 128:256] + sq[:, 256:384] + sq[:, 384:512] + sq[:, 512:640]
-            ACC[...] += _dot(x, W[r])
-            return carry
-
-        lax.fori_loop(0, 8, chunk, 0)
+            sq = sq[:, :128] + sq[:, 128:256] + sq[:, 256:384] + sq[:, 384:512] + sq[:, 512:640]
+            part = _dot(x, W[r])
+            if r:
+                SS[...] += sq
+                ACC[...] += part
+            else:
+                SS[...] = sq
+                ACC[...] = part
 
     def norms(s):
         inv = lax.rsqrt(jnp.sum(SS[...], axis=-1, keepdims=True) * (1.0 / 5120) + EPS)
@@ -139,38 +181,32 @@
             for d in Y_ORDER:
                 r = 4 - d
                 for i, buf in enumerate((KB, VB)):
-                    cp = remote(
-                        buf.at[1, pl.ds(1024, 256)], buf.at[1, pl.ds(r * 256, 256)],
-                        n_s.at[i, d], n_r.at[i, r], y_peer(d),
+                    here = buf.at[1, pl.ds(r * 256, 256)]
+                    send(
+                        ("n", i, r), buf.at[1, pl.ds(1024, 256)], here,
+                        n_s.at[i, d], n_r.at[i, r], y_peer(d), here, n_r.at[i, r],
                     )
-                    cp.start()
-                    sends.append(cp)
         for h in range(3):
             cols = pl.ds(h * 128, 128)
             q = ACC[:, cols] * inv
             QG[s, 0, :, cols] = (q * lax.rsqrt(jnp.mean(q * q, axis=-1, keepdims=True) + EPS)).astype(BF)
         for j in (3, 2, 1):
-            cp = remote(QG.at[s, 0], QG.at[s, j], q_s.at[s, j], q_r.at[s, j], class_peer(j))
-            cp.start()
-            sends.append(cp)
+            send(("q", s, j), QG.at[s, 0], QG.at[s, j], q_s.at[s, j], q_r.at[s, j], class_peer(j), QG.at[s, j], q_r.at[s, j])
 
     def wait_queries(s):
         for j in (1, 2, 3):
-            remote(QG.at[s, 0], QG.at[s, j], q_s.at[s, j], q_r.at[s, j], class_peer(j)).wait_recv()
+            take("q", s, j)
 
     lane = lax.broadcasted_iota(jnp.int32, (256, 128), 1)
 
     def send_partials(s, h):
         for j in (3, 2, 1):
-            cp = remote(PS.at[s, h, j], PR.at[s, h, j], p_s.at[s, h, j], p_r.at[s, h, j], class_peer(j))
-            cp.start()
-            sends.append(cp)
-            cp = remote(ST.at[s, h, j], STR.at[s, h, j], t_s.at[s, h, j], t_r.at[s, h, j], class_peer(j))
-            cp.start()
-            sends.append(cp)
-
-    def attention_one():
-        for h in range(3):
+            for name, src, dst, ssem, rsem in (("p", PS, PR, p_s, p_r), ("t", ST, STR, t_s, t_r)):
+                at = (s, h, j)
+                send((name,) + at, src.at[at], dst.at[at], ssem.at[at], rsem.at[at], class_peer(j), dst.at[at], rsem.at[at])
+
+    def attention_one(h):
+        if True:
             cols = pl.ds(h * 128, 128)
 
             def per_class(j, carry):
@@ -225,8 +261,8 @@
 
     def merge(s, h):
         for j in (1, 2, 3):
-            remote(PS.at[s, h, j], PR.at[s, h, j], p_s.at[s, h, j], p_r.at[s, h, j], class_peer(j)).wait_recv()
-            remote(ST.at[s, h, j], STR.at[s, h, j], t_s.at[s, h, j], t_r.at[s, h, j], class_peer(j)).wait_recv()
+            take("p", s, h, j)
+            take("t", s, h, j)
         stats = [ST[s, h, 0]] + [STR[s, h, j] for j in (1, 2, 3)]
         cols = [jnp.concatenate([st] * 16, axis=0).T for st in stats]
         accs = [OWN[h]] + [PR[s, h, j].astype(F32) for j in (1, 2, 3)]
@@ -241,21 +277,10 @@
             total = sum(ls)
             acc = sum(accs)
         AG[s, h, :, pl.ds(0, 128)] = (acc / total).astype(BF)
-        for r in T_ORDER:
-            m = mirror(r)
-            cp = remote(
-                AG.at[s, h, :, pl.ds(0, 128)], AG.at[s, h, :, pl.ds(m * 128, 128)],
-                a_s.at[s, h, r], a_r.at[s, h, m], t_peer(r),
-            )
-            cp.start()
-            sends.append(cp)
 
     def out_head(s, h):
-        for r in T_ORDER:
-            remote(
-                AG.at[s, h, :, pl.ds(0, 128)], AG.at[s, h, :, pl.ds(r * 128, 128)],
-                a_s.at[s, h, r], a_r.at[s, h, r], t_peer(r),
-            ).wait_recv()
+        for r in (2, 6, 5, 3, 7):
+            take("a", s, h, r)
         part = _dot(AG[s, h], WOG[h].reshape(1024, 640))
         if h == 0:
             OACC[...] = part + X[s, 0].astype(F32)
@@ -271,73 +296,81 @@
         for r in T_ORDER:
             m = mirror(r)
             cols = pl.ds(pl.multiple_of(t_index(r) * 640, 640), 640)
-            cp = remote(wo.at[:, wo_rows(0), cols], WOG.at[:, m, wo_rows(0)], o1_s.at[r], o1_r.at[m], t_peer(r))
-            cp.start()
-            sends.append(cp)
+            send(
+                ("o1", r), wo.at[:, wo_rows(0), cols], WOG.at[:, m, wo_rows(0)], o1_s.at[r], o1_r.at[m], t_peer(r),
+                WOG.at[:, r, wo_rows(0)], o1_r.at[r],
+            )
 
     def wo_first_wait():
         for r in T_ORDER:
-            remote(
-                wo.at[:, wo_rows(0), pl.ds(0, 640)], WOG.at[:, r, wo_rows(0)], o1_s.at[r], o1_r.at[r], t_peer(r)
-            ).wait_recv()
+            take("o1", r)
 
     def wo_piece(yy):
         return WOG.at[:, pl.ds(1, 7), wo_rows(yy)]
 
     def wo_third(yy):
-        cp = remote(wo_piece(yy), wo_piece(yy), o3_s.at[yy], o3_r.at[yy], class_peer(1))
-        cp.start()
-        sends.append(cp)
+        rows = pl.ds(pl.multiple_of((((y + yy) % 4) * 2 + (1 - c)) * 16, 16), 16)
+        send(
+            ("o3", yy), wo_piece(yy), wo_piece(yy), o3_s.at[yy], o3_r.at[yy], class_peer(1),
+            WOG.at[:, pl.ds(1, 7), rows], o3_r.at[yy],
+        )
 
     def wo_second():
         for d in Y_ORDER:
-            cp = remote(wo_piece(0), wo_piece(0), o2_s.at[d], o2_r.at[4 - d], y_peer(d))
-            cp.start()
-            sends.append(cp)
+            r = 4 - d
+            send(("o2", r), wo_piece(0), wo_piece(0), o2_s.at[d], o2_r.at[r], y_peer(d), wo_piece(r), o2_r.at[r])
         wo_third(0)
 
     def wo_relay():
         for r in Y_ORDER:
-            remote(wo_piece(0), wo_piece(r), o2_s.at[r], o2_r.at[r], y_peer(r)).wait_recv()
+            take("o2", r)
             wo_third(r)
 
     def wo_last_wait():
         for yy in range(4):
-            rows = pl.ds(pl.multiple_of((((y + yy) % 4) * 2 + (1 - c)) * 16, 16), 16)
-            piece = WOG.at[:, pl.ds(1, 7), rows]
-            remote(piece, piece, o3_s.at[yy], o3_r.at[yy], class_peer(1)).wait_recv()
+            take("o3", yy)
         own_wo.wait()
 
     project(0)
-    start_latents(1)
-    wo_first()
     norms(0)
     own_k.wait()
     own_v.wait()
     for r in Y_ORDER:
-        for i, (src, buf) in enumerate(((sk, KB), (sv, VB))):
-            remote(src, buf.at[0, pl.ds(r * 256, 256)], c_s.at[i, r], c_r.at[i, r], y_peer(r)).wait_recv()
+        for i in range(2):
+            take("c", i, r)
     wait_queries(0)
-    attention_one()
-    wo_first_wait()
-    wo_second()
+    attention_one(0)
+    gather_pass_partner(*latents_at(1))
+    attention_one(1)
+    gather_pass_opposite(*latents_at(1))
+    attention_one(2)
     for h in range(3):
         merge(0, h)
     project(1)
     norms(1)
+    wo_first()
+    for h in range(3):
+        start_attended(0, h)
     wait_queries(1)
     attention_two(0)
+    for h in range(3):
+        gather_pass_partner(*attended_at(0, h))
+        gather_pass_opposite(*attended_at(0, h))
+    wo_first_wait()
+    wo_second()
+    for r in Y_ORDER:
+        for i in range(2):
+            take("n", i, r)
+        attention_two(r)
+    for h in range(3):
+        merge(1, h)
+        start_attended(1, h)
     wo_relay()
-    for r in Y_ORDER:
-        for i, buf in enumerate((KB, VB)):
-            remote(
-                buf.at[1, pl.ds(1024, 256)], buf.at[1, pl.ds(r * 256, 256)],
-                n_s.at[i, r], n_r.at[i, r], y_peer(r),
-            ).wait_recv()
-        attention_two(r)
+    for h in range(3):
+        gather_pass_partner(*attended_at(1, h))
+        gather_pass_opposite(*attended_at(1, h))
     wo_last_wait()
     for h in range(3):
-        merge(1, h)
         out_head(0, h)
     for h in range(3):
         out_head(1, h)

time: 163 us -> 128 us (0.79)
  Pallas kernels: 158 us -> 124 us
    pallas_call x1, Pallas kernels: 158 us -> 124 us  [_shards(): pl.pallas_call(_kernel, out_shape=(out, out), in_specs=[pl.BlockSpec(memo...]
where the time goes in v2:
time: 128 us
  Pallas kernels  124 us (97%)
  local copies, waits for them, and re-layouts  3.45 us (3%)
    pallas_call x1, Pallas kernels, _shards(): pl.pallas_call(_kernel, out_shape=(out, out), in_specs=[pl.BlockSpec(memo...  124 us
    unnamed x2, local copies, waits for them, and re-layouts  3.45 us

profile of v2, /device:TPU:0, one launch (start us, length us, event | category | flops | bytes accessed | tf_op | source)
XLA Modules:
  0.0 127.7 jit_solution(9881501206981529860)
XLA Ops:
  0.6 123.6 %patch_attention.1 = (bf16[256,640]{1,0:T(8,128)(2,1)}, bf16[256,640]{1,0:T(8,128)(2,1)}) custom-call(bf16[256,640]{1,0:T(8,128)(2,1)} %lat1.1, bf16[256,640]{1,0:T(8,128)(2,1)} %lat2.1, bf16[256,384]{1,0:T(8,128)(2,1)} %sk.1, bf16[256,384]{1,0:T(8,128)(2,1)} %sv.1, bf16[5120,384]{1,0:T(8,128)(2,1)} %wq.1, bf16[5120,384]{1,0:T(8,128)(2,1)} %wk.1, ...), custom_call_target="tpu_custom_call" | custom-call | flops 11299999744 | bytes 20000000 | tf_op jit(solution)/shard_map/patch_attention/pallas_call | solution.py:416
  124.2 1.7 %copy.12 = bf16[256,640]{1,0:T(8,128)(2,1)} copy(bf16[256,640]{1,0:T(8,128)(2,1)} %get-tuple-element.4) | data formatting | bytes 655360
  125.9 1.7 %copy.13 = bf16[256,640]{1,0:T(8,128)(2,1)} copy(bf16[256,640]{1,0:T(8,128)(2,1)} %get-tuple-element.5) | data formatting | bytes 655360

commit v3 on v2

--- a/solution.py
+++ b/solution.py
@@ -27,8 +27,8 @@
 def _kernel(
     lat1, lat2, sk, sv, wq, wk, wv, wo,
     out1, out2,
-    X, W, ACC, SS, QG, KB, VB, OWN, PS, PR, ST, STR, AG, WOG, OACC, A2, L2,
-    x_s, x_r, w_l, c_s, c_r, n_s, n_r, q_s, q_r, p_s, p_r, t_s, t_r, a_s, a_r,
+    X, W, ACC, SS, QG, KB, VB, LA, LM, CS, CR, CST, CRT, PS, PR, PST, PRT, AG, WOG, OACC,
+    x_s, x_r, w_l, c_s, c_r, n_s, n_r, q_s, q_r, p_s, p_r, t_s, t_r, g_s, g_r, u_s, u_r, a_s, a_r,
     o1_s, o1_r, o2_s, o2_r, o3_s, o3_r, l_s,
 ):
     lats = (lat1, lat2)
@@ -75,15 +75,21 @@
         pending.pop(key).wait_recv()
 
     bar = pltpu.get_barrier_semaphore()
-    peers = [y_peer(d) for d in Y_ORDER] + [class_peer(j) for j in (1, 2, 3)] + [t_peer(r) for r in range(1, 8)]
+    peers = [y_peer(d) for d in Y_ORDER] + [class_peer(j) for j in (1, 2)] + [t_peer(r) for r in range(1, 8)]
     for dev in peers:
         pl.semaphore_signal(bar, inc=1, device_id=dev, device_id_type=pl.DeviceIdType.MESH)
     pl.semaphore_wait(bar, len(peers))
 
     def gather_send(key, own, at, ssem, rsem):
-        for r in (1, 4, 2, 6):
+        for r in (2, 6, 1):
             m = mirror(r)
             send(key + (r,), own, at(m), ssem(r), rsem(m), t_peer(r), at(r), rsem(r))
+
+    def gather_pass_sides(key, at, ssem, rsem):
+        for r, half, to in ((2, 0, 6), (6, 1, 2)):
+            n = 4 + 4 * half
+            take(*key, r)
+            send(key + (n,), at(r, half), at(4, half), ssem(n), rsem(n), t_peer(to), at(4, half), rsem(n))
 
     def gather_pass_partner(key, at, ssem, rsem):
         take(*key, 1)
@@ -91,11 +97,19 @@
             send(key + (slot,), at(1), at(slot), ssem(slot), rsem(slot), t_peer(r), at(slot), rsem(slot))
 
     def gather_pass_opposite(key, at, ssem, rsem):
-        take(*key, 4)
-        send(key + (5,), at(4), at(5), ssem(5), rsem(5), t_peer(1), at(5), rsem(5))
+        for half in (0, 1):
+            n = 5 + 4 * half
+            take(*key, n - 1)
+            send(key + (n,), at(4, half), at(5, half), ssem(n), rsem(n), t_peer(1), at(5, half), rsem(n))
+
+    def half_rows(half):
+        return pl.ds(0, 256) if half is None else pl.ds(half * 128, 128)
 
     def latents_at(s):
-        return ("x", s), (lambda r: X.at[s, r]), (lambda r: x_s.at[s, r]), (lambda r: x_r.at[s, r])
+        return (
+            ("x", s), (lambda r, half=None: X.at[s, r, half_rows(half)]),
+            (lambda n: x_s.at[s, n]), (lambda n: x_r.at[s, n]),
+        )
 
     def start_latents(s):
         key, at, ssem, rsem = latents_at(s)
@@ -103,8 +117,8 @@
 
     def attended_at(s, h):
         return (
-            ("a", s, h), (lambda r: AG.at[s, h, :, pl.ds(r * 128, 128)]),
-            (lambda r: a_s.at[s, h, r]), (lambda r: a_r.at[s, h, r]),
+            ("a", s, h), (lambda r, half=None: AG.at[s, h, half_rows(half), pl.ds(r * 128, 128)]),
+            (lambda n: a_s.at[s, h, n]), (lambda n: a_r.at[s, h, n]),
         )
 
     def start_attended(s, h):
@@ -139,16 +153,14 @@
     own_wo = pltpu.make_async_copy(wo.at[:, :, own_cols], WOG.at[:, 0], l_s.at[2])
     own_wo.start()
 
-    def project(s):
-        if s == 0:
-            gather_pass_partner(*latents_at(0))
-            gather_pass_opposite(*latents_at(0))
-        for r in SLOTS:
+    def project(s, slots):
+        for r in slots:
             if r == 0:
                 own_lat[s].wait()
-            elif r not in (1, 4):
-                if s == 0 and r == SLOTS[-1]:
-                    start_latents(1)
+            elif r == 5:
+                take("x", s, 5)
+                take("x", s, 9)
+            elif r in (3, 7):
                 take("x", s, r)
             if s == 0:
                 for copy in w_copies[r]:
@@ -190,97 +202,80 @@
             cols = pl.ds(h * 128, 128)
             q = ACC[:, cols] * inv
             QG[s, 0, :, cols] = (q * lax.rsqrt(jnp.mean(q * q, axis=-1, keepdims=True) + EPS)).astype(BF)
-        for j in (3, 2, 1):
+        for j in (2, 1):
             send(("q", s, j), QG.at[s, 0], QG.at[s, j], q_s.at[s, j], q_r.at[s, j], class_peer(j), QG.at[s, j], q_r.at[s, j])
 
-    def wait_queries(s):
-        for j in (1, 2, 3):
-            take("q", s, j)
+    def pass_queries(s):
+        take("q", s, 2)
+        send(("q", s, 3), QG.at[s, 2], QG.at[s, 3], q_s.at[s, 3], q_r.at[s, 3], class_peer(1), QG.at[s, 3], q_r.at[s, 3])
 
     lane = lax.broadcasted_iota(jnp.int32, (256, 128), 1)
 
-    def send_partials(s, h):
-        for j in (3, 2, 1):
-            for name, src, dst, ssem, rsem in (("p", PS, PR, p_s, p_r), ("t", ST, STR, t_s, t_r)):
-                at = (s, h, j)
-                send((name,) + at, src.at[at], dst.at[at], ssem.at[at], rsem.at[at], class_peer(j), dst.at[at], rsem.at[at])
-
-    def attention_one(h):
-        if True:
-            cols = pl.ds(h * 128, 128)
-
-            def per_class(j, carry):
-                start = pl.multiple_of(jnp.where(j == 0, 0, 256), 256)
-                q = QG[0, j, :, cols]
-                sc = _dot_nt(q, KB[0, pl.ds(start, 1024), cols])
-                m = jnp.max(sc, axis=-1, keepdims=True)
-                p = jnp.exp2((sc - m) * C)
-                l = jnp.sum(p, axis=-1, keepdims=True)
-                a = _dot(p.astype(BF), VB[0, pl.ds(start, 1024), cols])
-                PS[0, h, j] = a.astype(BF)
-                both = jnp.where(lane == 0, l, m)
-                ST[0, h, j] = both.T[:8]
-
-                @pl.when(j == 0)
-                def _():
-                    OWN[h] = a
-
-                return carry
-
-            lax.fori_loop(0, 4, per_class, 0)
-            send_partials(0, h)
-
-    def attention_two(part):
-        first = part == 0
-        for h in range(3):
-            cols = pl.ds(h * 128, 128)
-            if first:
-                blocks = ((0, 1, 0), (1, 3, 1024))
-            else:
-                blocks = ((0, 4, part * 256),)
-            for j0, nj, row in blocks:
-                q = QG[1, pl.ds(j0, nj), :, cols].reshape(nj * 256, 128)
-                p = jnp.exp2(_dot_nt(q, KB[1, pl.ds(row, 256), cols]) * C)
-                l = p[:, :128] + p[:, 128:]
-                a = _dot(p.astype(BF), VB[1, pl.ds(row, 256), cols])
-                rows = pl.ds(j0 * 256, nj * 256)
-                if first:
-                    A2[h, rows] = a
-                    L2[h, rows] = l
-                else:
-                    A2[h, rows] += a
-                    L2[h, rows] += l
-            if part == Y_ORDER[-1]:
-                OWN[h] = A2[h, pl.ds(0, 256)]
-                for j in range(4):
-                    rows = pl.ds(j * 256, 256)
-                    PS[1, h, j] = A2[h, rows].astype(BF)
-                    l = jnp.sum(L2[h, rows], axis=-1, keepdims=True)
-                    ST[1, h, j] = jnp.broadcast_to(l, (256, 128)).T[:8]
-                send_partials(1, h)
+    def pack(l, m):
+        return jnp.where(lane == 0, l, m)
+
+    def unpack(st):
+        both = jnp.concatenate([st] * 16, axis=0).T
+        return both[:, 0:1], both[:, 1:2]
+
+    def attend(s, h, j):
+        cols = pl.ds(h * 128, 128)
+        rows = pl.ds(0 if j == 0 else 256, 1024)
+        sc = _dot_nt(QG[s, j, :, cols], KB[s, rows, cols])
+        if s == 0:
+            m = jnp.max(sc, axis=-1, keepdims=True)
+            p = jnp.exp2((sc - m) * C)
+        else:
+            m = 0.0
+            p = jnp.exp2(sc * C)
+        l = jnp.sum(p, axis=-1, keepdims=True)
+        a = _dot(p.astype(BF), VB[s, rows, cols])
+        if j in (0, 2):
+            LA[s, h, j // 2] = a
+            LM[s, h, j // 2] = pack(l, m)
+        else:
+            at = (s, h, j // 2)
+            CS[at] = a
+            CST[at] = pack(l, m).T[:8]
+            for name, src, dst, ssem, rsem in (("g", CS, CR, g_s, g_r), ("u", CST, CRT, u_s, u_r)):
+                send((name,) + at, src.at[at], dst.at[at], ssem.at[at], rsem.at[at], class_peer(1), dst.at[at], rsem.at[at])
+
+    def add_up(s, parts):
+        accs, ls, ms = zip(*parts)
+        if s == 1:
+            return sum(accs), sum(ls), 0.0
+        top = functools.reduce(jnp.maximum, ms)
+        ws = [jnp.exp2((m - top) * C) for m in ms]
+        return sum(w * a for w, a in zip(ws, accs)), sum(w * l for w, l in zip(ws, ls)), top
+
+    def local(s, h, k):
+        both = LM[s, h, k]
+        return LA[s, h, k], both[:, 0:1], both[:, 1:2]
+
+    def from_core(s, h, k):
+        take("g", s, h, k)
+        take("u", s, h, k)
+        return (CR[s, h, k],) + unpack(CRT[s, h, k])
+
+    def combine(s, h):
+        a, l, m = add_up(s, [local(s, h, 1), from_core(s, h, 1)])
+        at = (s, h)
+        PS[at] = a.astype(BF)
+        PST[at] = pack(l, m).T[:8]
+        for name, src, dst, ssem, rsem in (("p", PS, PR, p_s, p_r), ("t", PST, PRT, t_s, t_r)):
+            send((name,) + at, src.at[at], dst.at[at], ssem.at[at], rsem.at[at], class_peer(2), dst.at[at], rsem.at[at])
 
     def merge(s, h):
-        for j in (1, 2, 3):
-            take("p", s, h, j)
-            take("t", s, h, j)
-        stats = [ST[s, h, 0]] + [STR[s, h, j] for j in (1, 2, 3)]
-        cols = [jnp.concatenate([st] * 16, axis=0).T for st in stats]
-        accs = [OWN[h]] + [PR[s, h, j].astype(F32) for j in (1, 2, 3)]
-        ls = [st[:, 0:1] for st in cols]
-        if s == 0:
-            ms = [st[:, 1:2] for st in cols]
-            top = functools.reduce(jnp.maximum, ms)
-            ws = [jnp.exp2((m - top) * C) for m in ms]
-            total = sum(w * l for w, l in zip(ws, ls))
-            acc = sum(w * a for w, a in zip(ws, accs))
-        else:
-            total = sum(ls)
-            acc = sum(accs)
-        AG[s, h, :, pl.ds(0, 128)] = (acc / total).astype(BF)
+        near = [local(s, h, 0), from_core(s, h, 0)]
+        take("p", s, h)
+        take("t", s, h)
+        a, l, _ = add_up(s, near + [(PR[s, h].astype(F32),) + unpack(PRT[s, h])])
+        AG[s, h, :, pl.ds(0, 128)] = (a / l).astype(BF)
+        start_attended(s, h)
 
     def out_head(s, h):
-        for r in (2, 6, 5, 3, 7):
-            take("a", s, h, r)
+        for n in (5, 9, 3, 7):
+            take("a", s, h, n)
         part = _dot(AG[s, h], WOG[h].reshape(1024, 640))
         if h == 0:
             OACC[...] = part + X[s, 0].astype(F32)
@@ -331,43 +326,70 @@
             take("o3", yy)
         own_wo.wait()
 
-    project(0)
+    gather_pass_sides(*latents_at(0))
+    gather_pass_partner(*latents_at(0))
+    project(0, (0, 1, 2, 6))
+    gather_pass_opposite(*latents_at(0))
+    project(0, (4, 3))
+    start_latents(1)
+    project(0, (7, 5))
     norms(0)
     own_k.wait()
     own_v.wait()
     for r in Y_ORDER:
         for i in range(2):
             take("c", i, r)
-    wait_queries(0)
-    attention_one(0)
+    for h in range(3):
+        attend(0, h, 0)
+    gather_pass_sides(*latents_at(1))
     gather_pass_partner(*latents_at(1))
-    attention_one(1)
+    pass_queries(0)
+    project(1, (0, 1, 2, 6))
     gather_pass_opposite(*latents_at(1))
-    attention_one(2)
-    for h in range(3):
-        merge(0, h)
-    project(1)
+    take("q", 0, 1)
+    for h in range(3):
+        attend(0, h, 1)
+    take("q", 0, 3)
+    for h in range(3):
+        attend(0, h, 3)
+        attend(0, h, 2)
+    for h in range(3):
+        combine(0, h)
+    project(1, (4, 3))
+    wo_first()
+    project(1, (7, 5))
     norms(1)
-    wo_first()
-    for h in range(3):
-        start_attended(0, h)
-    wait_queries(1)
-    attention_two(0)
-    for h in range(3):
-        gather_pass_partner(*attended_at(0, h))
-        gather_pass_opposite(*attended_at(0, h))
-    wo_first_wait()
-    wo_second()
     for r in Y_ORDER:
         for i in range(2):
             take("n", i, r)
-        attention_two(r)
+    for h in range(3):
+        attend(1, h, 0)
+    take("q", 1, 1)
+    for h in range(3):
+        attend(1, h, 1)
+    pass_queries(1)
+    for h in range(3):
+        merge(0, h)
+    wo_first_wait()
+    wo_second()
+    take("q", 1, 3)
+    for h in range(3):
+        attend(1, h, 3)
+        attend(1, h, 2)
+    for h in range(3):
+        combine(1, h)
+    for h in range(3):
+        gather_pass_sides(*attended_at(0, h))
+        gather_pass_partner(*attended_at(0, h))
     for h in range(3):
         merge(1, h)
-        start_attended(1, h)
+    for h in range(3):
+        gather_pass_opposite(*attended_at(0, h))
+    for h in range(3):
+        gather_pass_sides(*attended_at(1, h))
+        gather_pass_partner(*attended_at(1, h))
     wo_relay()
     for h in range(3):
-        gather_pass_partner(*attended_at(1, h))
         gather_pass_opposite(*attended_at(1, h))
     wo_last_wait()
     for h in range(3):
@@ -389,24 +411,29 @@
         vm((2, 4, 256, 384), BF),
         vm((2, 1280, 384), BF),
         vm((2, 1280, 384), BF),
-        vm((3, 256, 128), F32),
-        vm((2, 3, 4, 256, 128), BF),
-        vm((2, 3, 4, 256, 128), BF),
-        vm((2, 3, 4, 8, 256), F32),
-        vm((2, 3, 4, 8, 256), F32),
+        vm((2, 3, 2, 256, 128), F32),
+        vm((2, 3, 2, 256, 128), F32),
+        vm((2, 3, 2, 256, 128), F32),
+        vm((2, 3, 2, 256, 128), F32),
+        vm((2, 3, 2, 8, 256), F32),
+        vm((2, 3, 2, 8, 256), F32),
+        vm((2, 3, 256, 128), BF),
+        vm((2, 3, 256, 128), BF),
+        vm((2, 3, 8, 256), F32),
+        vm((2, 3, 8, 256), F32),
         vm((2, 3, 256, 1024), BF),
         vm((3, 8, 128, 640), BF),
         vm((256, 640), F32),
-        vm((3, 1024, 128), F32),
-        vm((3, 1024, 128), F32),
-        dma((2, 8)), dma((2, 8)),
+        dma((2, 10)), dma((2, 10)),
         dma((8, 3)),
         dma((2, 4)), dma((2, 4)),
         dma((2, 4)), dma((2, 4)),
         dma((2, 4)), dma((2, 4)),
-        dma((2, 3, 4)), dma((2, 3, 4)),
-        dma((2, 3, 4)), dma((2, 3, 4)),
-        dma((2, 3, 8)), dma((2, 3, 8)),
+        dma((2, 3)), dma((2, 3)),
+        dma((2, 3)), dma((2, 3)),
+        dma((2, 3, 2)), dma((2, 3, 2)),
+        dma((2, 3, 2)), dma((2, 3, 2)),
+        dma((2, 3, 10)), dma((2, 3, 10)),
         dma((8,)), dma((8,)),
         dma((4,)), dma((4,)),
         dma((4,)), dma((4,)),

time: 128 us -> 101 us (0.79)
  Pallas kernels: 124 us -> 96.3 us
    pallas_call x1, Pallas kernels: 124 us -> 96.3 us  [_shards(): pl.pallas_call(_kernel, out_shape=(out, out), in_specs=[pl.BlockSpec(memo...]
where the time goes in v3:
time: 101 us; the launch traced here: 100 us
  Pallas kernels  96.3 us (95%)
  local copies, waits for them, and re-layouts  3.45 us (3%)
    pallas_call x1, Pallas kernels, _shards(): pl.pallas_call(_kernel, out_shape=(out, out), in_specs=[pl.BlockSpec(memo...  96.3 us
    unnamed x2, local copies, waits for them, and re-layouts  3.45 us

profile of v3, /device:TPU:0, one launch (start us, length us, event | category | flops | bytes accessed | tf_op | source)
XLA Modules:
  0.0 100.4 jit_solution(7614169947899654896)
XLA Ops:
  0.6 96.3 %patch_attention.1 = (bf16[256,640]{1,0:T(8,128)(2,1)}, bf16[256,640]{1,0:T(8,128)(2,1)}) custom-call(bf16[256,640]{1,0:T(8,128)(2,1)} %lat1.1, bf16[256,640]{1,0:T(8,128)(2,1)} %lat2.1, bf16[256,384]{1,0:T(8,128)(2,1)} %sk.1, bf16[256,384]{1,0:T(8,128)(2,1)} %sv.1, bf16[5120,384]{1,0:T(8,128)(2,1)} %wq.1, bf16[5120,384]{1,0:T(8,128)(2,1)} %wk.1, ...), custom_call_target="tpu_custom_call" | custom-call | flops 11299999744 | bytes 20000000 | tf_op jit(solution)/shard_map/patch_attention/pallas_call | solution.py:443
  97.0 1.7 %copy.12 = bf16[256,640]{1,0:T(8,128)(2,1)} copy(bf16[256,640]{1,0:T(8,128)(2,1)} %get-tuple-element.4) | data formatting | bytes 655360
  98.7 1.7 %copy.13 = bf16[256,640]{1,0:T(8,128)(2,1)} copy(bf16[256,640]{1,0:T(8,128)(2,1)} %get-tuple-element.5) | data formatting | bytes 655360

commit v4 on v3

v4 whole, which is shorter than its diff:
```python
import functools
import math

import jax
import jax.numpy as jnp
from jax import lax
from jax.experimental import pallas as pl
from jax.experimental.pallas import tpu as pltpu
from jax.sharding import PartitionSpec as P

HD = 128
EPS = 1e-06
C = math.log2(math.e) / math.sqrt(HD)
BF = jnp.bfloat16
F32 = jnp.float32
Y_ORDER = (1, 3, 2)


def _dot(a, b):
    return jnp.dot(a, b, preferred_element_type=F32)


def _dot_nt(a, b):
    return lax.dot_general(a, b, (((1,), (1,)), ((), ())), preferred_element_type=F32)


def _kernel(
    lat1, lat2, sk, sv, wq, wk, wv, wo,
    out1, out2,
    X, W, ACC, SS, QG, KB, VB, LA, CS, CR, PS, PR, PST, PRT, AG, WOG, OACC,
    x_s, x_r, w_l, c_s, c_r, n_s, n_r, q_s, q_r, p_s, p_r, t_s, t_r, g_s, g_r, a_s, a_r,
    o1_s, o1_r, o2_s, o2_r, o3_s, o3_r, l_s,
):
    lats = (lat1, lat2)
    patch = lax.axis_index("patch")
    tens = lax.axis_index("tensor")
    xl, y, c = patch // 8, (patch // 2) % 4, patch % 2
    z, xh = tens // 2, tens % 2

    def y_peer(d):
        return (xl * 8 + ((y + d) % 4) * 2 + c, tens)

    def class_peer(j):
        nc = (c + j % 2) % 2
        nx = (xl + j // 2) % 2
        return (nx * 8 + y * 2 + nc, tens)

    def t_index(r):
        return ((z + r // 2) % 4) * 2 + (xh + r % 2) % 2

    def t_peer(r):
        return (patch, t_index(r))

    def mirror(r):
        return ((4 - r // 2) % 4) * 2 + r % 2

    def remote(src, dst, ssem, rsem, dev):
        return pltpu.make_async_remote_copy(
            src_ref=src, dst_ref=dst, send_sem=ssem, recv_sem=rsem,
            device_id=dev, device_id_type=pl.DeviceIdType.MESH,
        )

    T_ORDER = (1, 2, 6, 3, 7, 4, 5)
    SLOTS = (0, 1, 2, 6, 4, 3, 7, 5)
    PLACE = {r: i for i, r in enumerate(SLOTS)}

    def each_head(body):
        def step(h, carry):
            body(h)
            return carry

        lax.fori_loop(0, 3, step, 0)

    sends = []
    pending = {}

    def send(key, src, dst, ssem, rsem, dev, here, here_sem):
        cp = remote(src, dst, ssem, rsem, dev)
        cp.start()
        sends.append(cp)
        pending[key] = remote(here, here, here_sem, here_sem, t_peer(1))

    def take(*key):
        pending.pop(key).wait_recv()

    bar = pltpu.get_barrier_semaphore()
    peers = [y_peer(d) for d in Y_ORDER] + [class_peer(j) for j in (1, 2)] + [t_peer(r) for r in range(1, 8)]
    for dev in peers:
        pl.semaphore_signal(bar, inc=1, device_id=dev, device_id_type=pl.DeviceIdType.MESH)
    pl.semaphore_wait(bar, len(peers))

    OWN = ((0, None, 2, 6), (0, None, 6, 2), (0, None, 1, 1))
    SIDES = ((2, 0, 6, 4), (6, 1, 2, 4))
    PARTNER = ((1, None, 2, 7), (1, None, 6, 3))
    OPPOSITE = ((4, 0, 1, 5), (4, 1, 1, 5))

    def att_at(s, h, slot, half):
        return AG.at[s, h, half_rows(half), pl.ds(slot * 128, 128)]

    def att_copy(s, h, hop):
        slot, half, to, there = hop
        n = there + (4 if half else 0)
        return remote(att_at(s, h, slot, half), att_at(s, h, there, half), a_s.at[s, h, n], a_r.at[s, h, n], t_peer(to))

    def att_take(s, h, slot, half=None):
        n = slot + (4 if half else 0)
        here = att_at(s, h, slot, half)
        remote(here, here, a_s.at[s, h, n], a_r.at[s, h, n], t_peer(1)).wait_recv()

    def att_pass(s, h, hops, needs):
        for slot, half in needs:
            att_take(s, h, slot, half)
        for hop in hops:
            att_copy(s, h, hop).start()

    def att_first(s, h):
        att_pass(s, h, SIDES, ((2, None), (6, None)))
        att_pass(s, h, PARTNER, ((1, None),))

    def att_second(s, h):
        att_pass(s, h, OPPOSITE, ((4, 0), (4, 1)))

    def half_rows(half):
        return pl.ds(0, 256) if half is None else pl.ds(half * 128, 128)

    def lat_piece(s, slot, half):
        return X.at[s, PLACE[slot], half_rows(half)]

    def lat_send(s, src, to, slot, half):
        n = 2 * slot + half
        here = lat_piece(s, slot, half)
        send(("x", s, slot, half), src, here, x_s.at[s, n], x_r.at[s, n], t_peer(to), here, x_r.at[s, n])

    def start_latents(s):
        for r, half in ((2, 1), (6, 0), (1, 0), (2, 0), (6, 1), (1, 1)):
            lat_send(s, lats[s].at[half_rows(half)], r, mirror(r), half)

    def lat_sides(s):
        for slot, half, to in ((2, 0, 6), (6, 1, 2)):
            take("x", s, slot, half)
            lat_send(s, lat_piece(s, slot, half), to, 4, half)

    def lat_partner(s, half):
        take("x", s, 1, half)
        for to, slot in ((2, 7), (6, 3)):
            lat_send(s, lat_piece(s, 1, half), to, slot, half)

    def lat_opposite(s):
        for half in (0, 1):
            take("x", s, 4, half)
            lat_send(s, lat_piece(s, 4, half), 1, 5, half)

    def lat_opposite_z(s):
        for slot, half, to in ((3, 0, 6), (7, 1, 2)):
            take("x", s, slot, half)
            lat_send(s, lat_piece(s, slot, half), to, 5, half)

    start_latents(0)
    own_lat = [pltpu.make_async_copy(lats[s], X.at[s, 0], x_r.at[s, 0]) for s in (0, 1)]
    for cp in own_lat:
        cp.start()

    own_k = pltpu.make_async_copy(sk, KB.at[0, pl.ds(1024, 256)], l_s.at[0])
    own_v = pltpu.make_async_copy(sv, VB.at[0, pl.ds(1024, 256)], l_s.at[1])
    own_k.start()
    own_v.start()
    for d in Y_ORDER:
        r = 4 - d
        for i, (src, buf) in enumerate(((sk, KB), (sv, VB))):
            here = pl.ds(r * 256, 256)
            send(("c", i, r), src, buf.at[0, here], c_s.at[i, d], c_r.at[i, r], y_peer(d), buf.at[0, here], c_r.at[i, r])

    w_copies = {}
    for r in SLOTS:
        w_copies[r] = []
        rows = pl.ds(pl.multiple_of(t_index(r) * 640, 640), 640)
        for k, w in enumerate((wq, wk, wv)):
            copy = pltpu.make_async_copy(w.at[rows], W.at[PLACE[r], :, pl.ds(k * 384, 384)], w_l.at[r, k])
            copy.start()
            w_copies[r].append(copy)

    own_cols = pl.ds(pl.multiple_of(tens * 640, 640), 640)
    own_wo = pltpu.make_async_copy(wo.at[:, :, own_cols], WOG.at[:, 0], l_s.at[2])
    own_wo.start()

    def project(s, first, end):
        for r in SLOTS[first:end]:
            if r == 0:
                own_lat[s].wait()
            for half in (0, 1):
                if ("x", s, r, half) in pending:
                    take("x", s, r, half)
            if s == 0:
                for copy in w_copies[r]:
                    copy.wait()
        if first == 0:
            SS[...] = jnp.zeros_like(SS)
            ACC[...] = jnp.zeros_like(ACC)

        def chunk(i, carry):
            x = X[s, i]
            xf = x.astype(F32)
            sq = xf * xf
            SS[...] += sq[:, :128] + sq[:, 128:256] + sq[:, 256:384] + sq[:, 384:512] + sq[:, 512:640]
            ACC[...] += _dot(x, W[i])
            return carry

        lax.fori_loop(first, end, chunk, 0)

    def head_cols(h, base=0):
        return pl.ds(pl.multiple_of(base + h * 128, 128), 128)

    def norms(s):
        inv = lax.rsqrt(jnp.sum(SS[...], axis=-1, keepdims=True) * (1.0 / 5120) + EPS)

        def unit(x):
            x = x * inv
            return (x * lax.rsqrt(jnp.mean(x * x, axis=-1, keepdims=True) + EPS)).astype(BF)

        @each_head
        def _(h):
            cols = head_cols(h)
            k = unit(ACC[:, head_cols(h, 384)])
            v = (ACC[:, head_cols(h, 768)] * inv).astype(BF)
            KB[s, pl.ds(0, 256), cols] = k
            VB[s, pl.ds(0, 256), cols] = v
            if s == 0:
                KB[1, pl.ds(1024, 256), cols] = k
                VB[1, pl.ds(1024, 256), cols] = v

        if s == 0:
            for d in Y_ORDER:
                r = 4 - d
                for i, buf in enumerate((KB, VB)):
                    here = buf.at[1, pl.ds(r * 256, 256)]
                    send(
                        ("n", i, r), buf.at[1, pl.ds(1024, 256)], here,
                        n_s.at[i, d], n_r.at[i, r], y_peer(d), here, n_r.at[i, r],
                    )

        @each_head
        def _(h):
            QG[s, 0, :, head_cols(h)] = unit(ACC[:, head_cols(h)])

        for j in (2, 1):
            send(("q", s, j), QG.at[s, 0], QG.at[s, j], q_s.at[s, j], q_r.at[s, j], class_peer(j), QG.at[s, j], q_r.at[s, j])

    def pass_queries(s):
        take("q", s, 2)
        send(("q", s, 3), QG.at[s, 2], QG.at[s, 3], q_s.at[s, 3], q_r.at[s, 3], class_peer(1), QG.at[s, 3], q_r.at[s, 3])

    lane = lax.broadcasted_iota(jnp.int32, (256, 128), 1)

    def pack(l, m):
        return jnp.where(lane == 0, l, m)

    def unpack(st):
        both = jnp.concatenate([st] * 16, axis=0).T
        return both[:, 0:1], both[:, 1:2]

    def core_copy(s, h, k):
        at = (s, h, k)
        return remote(CS.at[at], CR.at[at], g_s.at[at], g_r.at[at], class_peer(1))

    def x_copies(s, h):
        at = (s, h)
        return (
            remote(PS.at[at], PR.at[at], p_s.at[at], p_r.at[at], class_peer(2)),
            remote(PST.at[at], PRT.at[at], t_s.at[at], t_r.at[at], class_peer(2)),
        )

    def attend(s, h, j):
        cols = head_cols(h)
        rows = [pl.ds(0 if i == 0 else 256, 1024) for i in (j, j + 1)]
        sc = [_dot_nt(QG[s, j + i, :, cols], KB[s, rows[i], cols]) for i in (0, 1)]
        m = [jnp.max(x, axis=-1, keepdims=True) if s == 0 else 0.0 for x in sc]
        p = [jnp.exp2((x - y) * C) if s == 0 else jnp.exp2(x * C) for x, y in zip(sc, m)]
        l = [jnp.sum(x, axis=-1, keepdims=True) for x in p]
        a = [_dot(p[i].astype(BF), VB[s, rows[i], cols]) for i in (0, 1)]
        k = j // 2
        CS[s, h, k, 0] = a[1]
        CS[s, h, k, 1] = pack(l[1], m[1])
        core_copy(s, h, k).start()
        LA[s, h, k, 0] = a[0]
        LA[s, h, k, 1] = pack(l[0], m[0])

    def add_up(s, parts):
        accs, ls, ms = zip(*parts)
        if s == 1:
            return sum(accs), sum(ls), 0.0
        top = functools.reduce(jnp.maximum, ms)
        ws = [jnp.exp2((m - top) * C) for m in ms]
        return sum(w * a for w, a in zip(ws, accs)), sum(w * l for w, l in zip(ws, ls)), top

    def near(s, h, k):
        core_copy(s, h, k).wait_recv()
        return [(ref[s, h, k, 0], ref[s, h, k, 1][:, 0:1], ref[s, h, k, 1][:, 1:2]) for ref in (LA, CR)]

    def combine(s, h):
        a, l, m = add_up(s, near(s, h, 1))
        PS[s, h] = a.astype(BF)
        PST[s, h] = pack(l, m).T[:8]
        for copy in x_copies(s, h):
            copy.start()

    def merge(s, h):
        parts = near(s, h, 0)
        for copy in x_copies(s, h):
            copy.wait_recv()
        a, l, _ = add_up(s, parts + [(PR[s, h].astype(F32),) + unpack(PRT[s, h])])
        AG[s, h, :, pl.ds(0, 128)] = (a / l).astype(BF)
        att_pass(s, h, OWN, ())

    def out_head(s, h):
        for slot, half in ((5, 0), (5, 1), (3, None), (7, None)):
            att_take(s, h, slot, half)
        OACC[...] += _dot(AG[s, h], WOG[h].reshape(1024, 640))

    def output(s):
        OACC[...] = jnp.zeros_like(OACC)
        each_head(functools.partial(out_head, s))
        (out1, out2)[s][...] = OACC[...]

    def settle(s):
        @each_head
        def _(h):
            for k in (0, 1):
                core_copy(s, h, k).wait_send()
            for copy in x_copies(s, h):
                copy.wait_send()
            for hop in OWN + SIDES + PARTNER + OPPOSITE:
                att_copy(s, h, hop).wait_send()

    def wo_rows(yy):
        return pl.ds(pl.multiple_of((((y + yy) % 4) * 2 + c) * 16, 16), 16)

    def wo_first():
        for r in T_ORDER:
            m = mirror(r)
            cols = pl.ds(pl.multiple_of(t_index(r) * 640, 640), 640)
            send(
                ("o1", r), wo.at[:, wo_rows(0), cols], WOG.at[:, m, wo_rows(0)], o1_s.at[r], o1_r.at[m], t_peer(r),
                WOG.at[:, r, wo_rows(0)], o1_r.at[r],
            )

    def wo_first_wait():
        for r in T_ORDER:
            take("o1", r)

    def wo_piece(yy):
        return WOG.at[:, pl.ds(1, 7), wo_rows(yy)]

    def wo_third(yy):
        rows = pl.ds(pl.multiple_of((((y + yy) % 4) * 2 + (1 - c)) * 16, 16), 16)
        send(
            ("o3", yy), wo_piece(yy), wo_piece(yy), o3_s.at[yy], o3_r.at[yy], class_peer(1),
            WOG.at[:, pl.ds(1, 7), rows], o3_r.at[yy],
        )

    def wo_second():
        for d in Y_ORDER:
            r = 4 - d
            send(("o2", r), wo_piece(0), wo_piece(0), o2_s.at[d], o2_r.at[r], y_peer(d), wo_piece(r), o2_r.at[r])
        wo_third(0)

    def wo_relay():
        for r in Y_ORDER:
            take("o2", r)
            wo_third(r)

    def wo_last_wait():
        for yy in range(4):
            take("o3", yy)
        own_wo.wait()

    def heads(fn, *args):
        each_head(lambda h: fn(args[0], h, *args[1:]))

    lat_sides(0)
    lat_partner(0, 0)
    lat_partner(0, 1)
    lat_opposite(0)
    wo_first()
    project(0, 0, 5)
    start_latents(1)
    project(0, 5, 8)
    norms(0)
    own_k.wait()
    own_v.wait()
    for r in Y_ORDER:
        for i in range(2):
            take("c", i, r)
    lat_sides(1)
    lat_partner(1, 0)
    take("q", 0, 1)
    heads(attend, 0, 0)
    lat_partner(1, 1)
    lat_opposite(1)
    pass_queries(0)
    project(1, 0, 4)
    take("q", 0, 3)
    heads(attend, 0, 2)
    wo_first_wait()
    wo_second()
    heads(combine, 0)
    project(1, 4, 8)
    norms(1)
    for r in Y_ORDER:
        for i in range(2):
            take("n", i, r)
    heads(merge, 0)
    take("q", 1, 1)
    heads(attend, 1, 0)
    pass_queries(1)
    heads(att_first, 0)
    take("q", 1, 3)
    heads(attend, 1, 2)
    heads(combine, 1)
    heads(merge, 1)
    heads(att_second, 0)
    heads(att_first, 1)
    wo_relay()
    heads(att_second, 1)
    settle(0)
    wo_last_wait()
    output(0)
    output(1)
    settle(1)
    for cp in sends:
        cp.wait_send()


def _shards(latent_first, latent_second, stale_keys, stale_values, w_query, w_key, w_value, w_output):
    dma = pltpu.SemaphoreType.DMA
    vm = pltpu.VMEM
    scratch = [
        vm((2, 8, 256, 640), BF),
        vm((8, 640, 1152), BF),
        vm((256, 1152), F32),
        vm((256, 128), F32),
        vm((2, 4, 256, 384), BF),
        vm((2, 1280, 384), BF),
        vm((2, 1280, 384), BF),
        vm((2, 3, 2, 2, 256, 128), F32),
        vm((2, 3, 2, 2, 256, 128), F32),
        vm((2, 3, 2, 2, 256, 128), F32),
        vm((2, 3, 256, 128), BF),
        vm((2, 3, 256, 128), BF),
        vm((2, 3, 8, 256), F32),
        vm((2, 3, 8, 256), F32),
        vm((2, 3, 256, 1024), BF),
        vm((3, 8, 128, 640), BF),
        vm((256, 640), F32),
        dma((2, 16)), dma((2, 16)),
        dma((8, 3)),
        dma((2, 4)), dma((2, 4)),
        dma((2, 4)), dma((2, 4)),
        dma((2, 4)), dma((2, 4)),
        dma((2, 3)), dma((2, 3)),
        dma((2, 3)), dma((2, 3)),
        dma((2, 3, 2)), dma((2, 3, 2)),
        dma((2, 3, 10)), dma((2, 3, 10)),
        dma((8,)), dma((8,)),
        dma((4,)), dma((4,)),
        dma((4,)), dma((4,)),
        dma((3,)),
    ]
    out = jax.ShapeDtypeStruct((256, 640), F32)
    sums = pl.pallas_call(
        _kernel,
        out_shape=(out, out),
        in_specs=[pl.BlockSpec(memory_space=pl.ANY)] * 8,
        out_specs=(pl.BlockSpec(memory_space=pltpu.VMEM),) * 2,
        scratch_shapes=scratch,
        compiler_params=pltpu.CompilerParams(
            collective_id=0, has_side_effects=True, vmem_limit_bytes=60 * 2**20
        ),
        cost_estimate=pl.CostEstimate(flops=11_300_000_000, bytes_accessed=20_000_000, transcendentals=6_300_000),
        name="patch_attention",
    )(
        latent_first, latent_second, stale_keys, stale_values,
        w_query, w_key, w_value, w_output.reshape(3, 128, 5120),
    )
    return tuple((x.astype(F32) + part).astype(BF) for x, part in zip((latent_first, latent_second), sums))


def solution(mesh):
    in_specs = (
        P("patch", "tensor"),
        P("patch", "tensor"),
        P("patch", "tensor"),
        P("patch", "tensor"),
        P(None, "tensor"),
        P(None, "tensor"),
        P(None, "tensor"),
        P("tensor", None),
    )
    out_specs = (P("patch", "tensor"), P("patch", "tensor"))
    return jax.shard_map(_shards, mesh=mesh, in_specs=in_specs, out_specs=out_specs, check_vma=False)
```

time: 101 us -> 98.1 us (0.971)
  local copies, waits for them, and re-layouts: 3.45 us -> 0.01 us
  other arithmetic: 0 us -> 2.23 us
  Pallas kernels: 96.3 us -> 95 us
    unnamed x2 -> x4, local copies, waits for them, and re-layouts: 3.45 us -> 0.01 us
    convert_element_type x0 -> x1, other arithmetic: none -> 2.23 us  [_shards(): (x.astype(F32) + part).astype(BF)]
    pallas_call x1, Pallas kernels: 96.3 us -> 95 us  [_shards(): pl.pallas_call(_kernel, out_shape=(out, out), in_specs=[pl.BlockSpec(memo...]
where the time goes in v4:
time: 98.1 us; the launch traced here: 98 us
  Pallas kernels  95 us (97%)
  other arithmetic  2.23 us (2%)
    pallas_call x1, Pallas kernels, _shards(): pl.pallas_call(_kernel, out_shape=(out, out), in_specs=[pl.BlockSpec(memo...  95 us
    convert_element_type x1, other arithmetic, _shards(): (x.astype(F32) + part).astype(BF)  2.23 us

profile of v4, /device:TPU:0, one launch (start us, length us, event | category | flops | bytes accessed | tf_op | source)
XLA Modules:
  0.0 98.0 jit_solution(10532534023999307470)
XLA Ops:
  0.6 0.0 copy-start
  0.6 0.0 copy-start.1
  0.7 95.0 %patch_attention.1 = (f32[256,640]{1,0:T(8,128)}, f32[256,640]{1,0:T(8,128)}) custom-call(bf16[256,640]{1,0:T(8,128)(2,1)} %lat1.1, bf16[256,640]{1,0:T(8,128)(2,1)} %lat2.1, bf16[256,384]{1,0:T(8,128)(2,1)} %sk.1, bf16[256,384]{1,0:T(8,128)(2,1)} %sv.1, bf16[5120,384]{1,0:T(8,128)(2,1)} %wq.1, bf16[5120,384]{1,0:T(8,128)(2,1)} %wk.1, bf16[5120,384]{1,0:T(8,128)(2,1)} %wv.1, ...), custom_call_target="tpu_custom_call" | custom-call | flops 11299999744 | bytes 20000000 | tf_op jit(solution)/shard_map/patch_attention/pallas_call | solution.py:469
  95.7 0.0 copy-done
  95.7 0.0 copy-done.1
  95.7 2.2 %add_convert_fusion = (bf16[256,640]{1,0:T(8,128)(2,1)}, bf16[256,640]{1,0:T(8,128)(2,1)}) fusion(f32[256,640]{1,0:T(8,128)} %get-tuple-element.5, bf16[256,640]{1,0:T(8,128)(2,1)S(1)} %copy-done.1, f32[256,640]{1,0:T(8,128)} %get-tuple-element.4, bf16[256,640]{1,0:T(8,128)(2,1)S(1)} %copy-done), kind=kLoop, calls=%fused_computation | loop fusion | flops 983040 | bytes 2621440 | tf_op jit(solution)/shard_map/convert_element_type | solution.py:484
Async XLA Ops:
  0.6 95.1 %copy-start = (bf16[256,640]{1,0:T(8,128)(2,1)S(1)}, bf16[256,640]{1,0:T(8,128)(2,1)}, u32[]{:S(2)}) copy-start(bf16[256,640]{1,0:T(8,128)(2,1)} %lat1.1) | copy-start | bytes 983044
  0.6 95.1 %copy-start.1 = (bf16[256,640]{1,0:T(8,128)(2,1)S(1)}, bf16[256,640]{1,0:T(8,128)(2,1)}, u32[]{:S(2)}) copy-start(bf16[256,640]{1,0:T(8,128)(2,1)} %lat2.1) | copy-start | bytes 983044

commit v5 on v4

--- a/solution.py
+++ b/solution.py
@@ -217,18 +217,20 @@
             x = x * inv
             return (x * lax.rsqrt(jnp.mean(x * x, axis=-1, keepdims=True) + EPS)).astype(BF)
 
-        @each_head
-        def _(h):
-            cols = head_cols(h)
-            k = unit(ACC[:, head_cols(h, 384)])
-            v = (ACC[:, head_cols(h, 768)] * inv).astype(BF)
-            KB[s, pl.ds(0, 256), cols] = k
-            VB[s, pl.ds(0, 256), cols] = v
-            if s == 0:
-                KB[1, pl.ds(1024, 256), cols] = k
-                VB[1, pl.ds(1024, 256), cols] = v
+        def keys_values():
+            @each_head
+            def _(h):
+                cols = head_cols(h)
+                k = unit(ACC[:, head_cols(h, 384)])
+                v = (ACC[:, head_cols(h, 768)] * inv).astype(BF)
+                KB[s, pl.ds(0, 256), cols] = k
+                VB[s, pl.ds(0, 256), cols] = v
+                if s == 0:
+                    KB[1, pl.ds(1024, 256), cols] = k
+                    VB[1, pl.ds(1024, 256), cols] = v
 
         if s == 0:
+            keys_values()
             for d in Y_ORDER:
                 r = 4 - d
                 for i, buf in enumerate((KB, VB)):
@@ -241,13 +243,25 @@
         @each_head
         def _(h):
             QG[s, 0, :, head_cols(h)] = unit(ACC[:, head_cols(h)])
-
-        for j in (2, 1):
-            send(("q", s, j), QG.at[s, 0], QG.at[s, j], q_s.at[s, j], q_r.at[s, j], class_peer(j), QG.at[s, j], q_r.at[s, j])
-
-    def pass_queries(s):
-        take("q", s, 2)
-        send(("q", s, 3), QG.at[s, 2], QG.at[s, 3], q_s.at[s, 3], q_r.at[s, 3], class_peer(1), QG.at[s, 3], q_r.at[s, 3])
+            for j in (2, 1):
+                q_copy(s, h, j).start()
+
+        if s == 1:
+            keys_values()
+
+    def q_copy(s, h, j):
+        cols = head_cols(h)
+        return remote(
+            QG.at[s, 2 if j == 3 else 0, :, cols], QG.at[s, j, :, cols],
+            q_s.at[s, j, h], q_r.at[s, j, h], class_peer(2 if j == 2 else 1),
+        )
+
+    def take_query(s, h, j):
+        q_copy(s, h, j).wait_recv()
+
+    def pass_query(s, h):
+        take_query(s, h, 2)
+        q_copy(s, h, 3).start()
 
     lane = lax.broadcasted_iota(jnp.int32, (256, 128), 1)
 
@@ -324,6 +338,8 @@
     def settle(s):
         @each_head
         def _(h):
+            for j in (1, 2, 3):
+                q_copy(s, h, j).wait_send()
             for k in (0, 1):
                 core_copy(s, h, k).wait_send()
             for copy in x_copies(s, h):
@@ -392,13 +408,13 @@
             take("c", i, r)
     lat_sides(1)
     lat_partner(1, 0)
-    take("q", 0, 1)
+    heads(take_query, 0, 1)
     heads(attend, 0, 0)
     lat_partner(1, 1)
     lat_opposite(1)
-    pass_queries(0)
+    heads(pass_query, 0)
     project(1, 0, 4)
-    take("q", 0, 3)
+    heads(take_query, 0, 3)
     heads(attend, 0, 2)
     wo_first_wait()
     wo_second()
@@ -409,13 +425,19 @@
         for i in range(2):
             take("n", i, r)
     heads(merge, 0)
-    take("q", 1, 1)
-    heads(attend, 1, 0)
-    pass_queries(1)
+    for h in range(3):
+        take_query(1, h, 1)
+        attend(1, h, 0)
+        if h:
+            pass_query(1, h - 1)
+    pass_query(1, 2)
+    for h in range(3):
+        take_query(1, h, 3)
+        attend(1, h, 2)
+        if h:
+            combine(1, h - 1)
+    combine(1, 2)
     heads(att_first, 0)
-    take("q", 1, 3)
-    heads(attend, 1, 2)
-    heads(combine, 1)
     heads(merge, 1)
     heads(att_second, 0)
     heads(att_first, 1)
@@ -455,7 +477,7 @@
         dma((8, 3)),
         dma((2, 4)), dma((2, 4)),
         dma((2, 4)), dma((2, 4)),
-        dma((2, 4)), dma((2, 4)),
+        dma((2, 4, 3)), dma((2, 4, 3)),
         dma((2, 3)), dma((2, 3)),
         dma((2, 3)), dma((2, 3)),
         dma((2, 3, 2)), dma((2, 3, 2)),

time: 98.1 us -> 96.5 us (0.984)
  Pallas kernels: 95 us -> 93.4 us
    pallas_call x1, Pallas kernels: 95 us -> 93.4 us  [_shards(): pl.pallas_call(_kernel, out_shape=(out, out), in_specs=[pl.BlockSpec(memo...]
where the time goes in v5:
time: 96.5 us; the launch traced here: 96.3 us
  Pallas kernels  93.4 us (97%)
  other arithmetic  2.23 us (2%)
    pallas_call x1, Pallas kernels, _shards(): pl.pallas_call(_kernel, out_shape=(out, out), in_specs=[pl.BlockSpec(memo...  93.4 us
    convert_element_type x1, other arithmetic, _shards(): (x.astype(F32) + part).astype(BF)  2.23 us

profile of v5, /device:TPU:0, one launch (start us, length us, event | category | flops | bytes accessed | tf_op | source)
XLA Modules:
  0.0 96.3 jit_solution(5934955524758830860)
XLA Ops:
  0.6 0.0 copy-start
  0.6 0.0 copy-start.1
  0.7 93.4 %patch_attention.1 = (f32[256,640]{1,0:T(8,128)}, f32[256,640]{1,0:T(8,128)}) custom-call(bf16[256,640]{1,0:T(8,128)(2,1)} %lat1.1, bf16[256,640]{1,0:T(8,128)(2,1)} %lat2.1, bf16[256,384]{1,0:T(8,128)(2,1)} %sk.1, bf16[256,384]{1,0:T(8,128)(2,1)} %sv.1, bf16[5120,384]{1,0:T(8,128)(2,1)} %wq.1, bf16[5120,384]{1,0:T(8,128)(2,1)} %wk.1, bf16[5120,384]{1,0:T(8,128)(2,1)} %wv.1, ...), custom_call_target="tpu_custom_call" | custom-call | flops 11299999744 | bytes 20000000 | tf_op jit(solution)/shard_map/patch_attention/pallas_call | solution.py:491
  94.1 0.0 copy-done
  94.1 0.0 copy-done.1
  94.1 2.2 %add_convert_fusion = (bf16[256,640]{1,0:T(8,128)(2,1)}, bf16[256,640]{1,0:T(8,128)(2,1)}) fusion(f32[256,640]{1,0:T(8,128)} %get-tuple-element.5, bf16[256,640]{1,0:T(8,128)(2,1)S(1)} %copy-done.1, f32[256,640]{1,0:T(8,128)} %get-tuple-element.4, bf16[256,640]{1,0:T(8,128)(2,1)S(1)} %copy-done), kind=kLoop, calls=%fused_computation | loop fusion | flops 983040 | bytes 2621440 | tf_op jit(solution)/shard_map/convert_element_type | solution.py:506
Async XLA Ops:
  0.6 93.4 %copy-start = (bf16[256,640]{1,0:T(8,128)(2,1)S(1)}, bf16[256,640]{1,0:T(8,128)(2,1)}, u32[]{:S(2)}) copy-start(bf16[256,640]{1,0:T(8,128)(2,1)} %lat1.1) | copy-start | bytes 983044
  0.6 93.4 %copy-start.1 = (bf16[256,640]{1,0:T(8,128)(2,1)S(1)}, bf16[256,640]{1,0:T(8,128)(2,1)}, u32[]{:S(2)}) copy-start(bf16[256,640]{1,0:T(8,128)(2,1)} %lat2.1) | copy-start | bytes 983044

commit v6 on v5

--- a/solution.py
+++ b/solution.py
@@ -328,12 +328,15 @@
     def out_head(s, h):
         for slot, half in ((5, 0), (5, 1), (3, None), (7, None)):
             att_take(s, h, slot, half)
-        OACC[...] += _dot(AG[s, h], WOG[h].reshape(1024, 640))
+        OACC[s] += _dot(AG[s, h], WOG[h].reshape(1024, 640))
+
+    def output_copy(s):
+        return pltpu.make_async_copy(OACC.at[s], (out1, out2)[s], l_s.at[3 + s])
 
     def output(s):
-        OACC[...] = jnp.zeros_like(OACC)
+        OACC[s] = jnp.zeros((256, 640), F32)
         each_head(functools.partial(out_head, s))
-        (out1, out2)[s][...] = OACC[...]
+        output_copy(s).start()
 
     def settle(s):
         @each_head
@@ -344,8 +347,12 @@
                 core_copy(s, h, k).wait_send()
             for copy in x_copies(s, h):
                 copy.wait_send()
-            for hop in OWN + SIDES + PARTNER + OPPOSITE:
+            for hop in OWN + SIDES + PARTNER:
                 att_copy(s, h, hop).wait_send()
+
+    def settle_last(s, h):
+        for hop in OPPOSITE:
+            att_copy(s, h, hop).wait_send()
 
     def wo_rows(yy):
         return pl.ds(pl.multiple_of((((y + yy) % 4) * 2 + c) * 16, 16), 16)
@@ -444,12 +451,16 @@
     wo_relay()
     heads(att_second, 1)
     settle(0)
+    heads(settle_last, 0)
+    for cp in sends:
+        cp.wait_send()
     wo_last_wait()
     output(0)
+    settle(1)
     output(1)
-    settle(1)
-    for cp in sends:
-        cp.wait_send()
+    heads(settle_last, 1)
+    output_copy(0).wait()
+    output_copy(1).wait()
 
 
 def _shards(latent_first, latent_second, stale_keys, stale_values, w_query, w_key, w_value, w_output):
@@ -472,7 +483,7 @@
         vm((2, 3, 8, 256), F32),
         vm((2, 3, 256, 1024), BF),
         vm((3, 8, 128, 640), BF),
-        vm((256, 640), F32),
+        vm((2, 256, 640), F32),
         dma((2, 16)), dma((2, 16)),
         dma((8, 3)),
         dma((2, 4)), dma((2, 4)),
@@ -485,14 +496,14 @@
         dma((8,)), dma((8,)),
         dma((4,)), dma((4,)),
         dma((4,)), dma((4,)),
-        dma((3,)),
+        dma((5,)),
     ]
     out = jax.ShapeDtypeStruct((256, 640), F32)
     sums = pl.pallas_call(
         _kernel,
         out_shape=(out, out),
         in_specs=[pl.BlockSpec(memory_space=pl.ANY)] * 8,
-        out_specs=(pl.BlockSpec(memory_space=pltpu.VMEM),) * 2,
+        out_specs=(pl.BlockSpec(memory_space=pl.ANY),) * 2,
         scratch_shapes=scratch,
         compiler_params=pltpu.CompilerParams(
             collective_id=0, has_side_effects=True, vmem_limit_bytes=60 * 2**20

time: 96.5 us -> 96.1 us (level)
  no operation moved by 1% of the time
where the time goes in v6:
time: 96.1 us; the launch traced here: 95.9 us
  Pallas kernels  93 us (97%)
  other arithmetic  2.23 us (2%)
    pallas_call x1, Pallas kernels, _shards(): pl.pallas_call(_kernel, out_shape=(out, out), in_specs=[pl.BlockSpec(memo...  93 us
    convert_element_type x1, other arithmetic, _shards(): (x.astype(F32) + part).astype(BF)  2.23 us

profile of v6, /device:TPU:0, one launch (start us, length us, event | category | flops | bytes accessed | tf_op | source)
XLA Modules:
  0.0 95.9 jit_solution(5421820640986740321)
XLA Ops:
  0.6 0.0 copy-start
  0.6 0.0 copy-start.1
  0.7 93.0 %patch_attention.1 = (f32[256,640]{1,0:T(8,128)}, f32[256,640]{1,0:T(8,128)}) custom-call(bf16[256,640]{1,0:T(8,128)(2,1)} %lat1.1, bf16[256,640]{1,0:T(8,128)(2,1)} %lat2.1, bf16[256,384]{1,0:T(8,128)(2,1)} %sk.1, bf16[256,384]{1,0:T(8,128)(2,1)} %sv.1, bf16[5120,384]{1,0:T(8,128)(2,1)} %wq.1, bf16[5120,384]{1,0:T(8,128)(2,1)} %wk.1, bf16[5120,384]{1,0:T(8,128)(2,1)} %wv.1, ...), custom_call_target="tpu_custom_call" | custom-call | flops 11299999744 | bytes 20000000 | tf_op jit(solution)/shard_map/patch_attention/pallas_call | solution.py:502
  93.7 0.0 copy-done
  93.7 0.0 copy-done.1
  93.7 2.2 %add_convert_fusion = (bf16[256,640]{1,0:T(8,128)(2,1)}, bf16[256,640]{1,0:T(8,128)(2,1)}) fusion(f32[256,640]{1,0:T(8,128)} %get-tuple-element.5, bf16[256,640]{1,0:T(8,128)(2,1)S(1)} %copy-done.1, f32[256,640]{1,0:T(8,128)} %get-tuple-element.4, bf16[256,640]{1,0:T(8,128)(2,1)S(1)} %copy-done), kind=kLoop, calls=%fused_computation | loop fusion | flops 983040 | bytes 2621440 | tf_op jit(solution)/shard_map/convert_element_type | solution.py:517
Async XLA Ops:
  0.6 93.0 %copy-start = (bf16[256,640]{1,0:T(8,128)(2,1)S(1)}, bf16[256,640]{1,0:T(8,128)(2,1)}, u32[]{:S(2)}) copy-start(bf16[256,640]{1,0:T(8,128)(2,1)} %lat1.1) | copy-start | bytes 983044
  0.6 93.0 %copy-start.1 = (bf16[256,640]{1,0:T(8,128)(2,1)S(1)}, bf16[256,640]{1,0:T(8,128)(2,1)}, u32[]{:S(2)}) copy-start(bf16[256,640]{1,0:T(8,128)(2,1)} %lat2.1) | copy-start | bytes 983044
